TPU v7x, 512 devices: a whole 4x4x16 slice. The times are simulated.
512 devices in a mesh: gx: 8 (over x, core), gy: 8 (over z_hi, y), gz: 8 (over z_lo).
Axes of the slice: x: 4, y: 4, z: 16 (z_hi: 2, z_lo: 8; z = z_hi * 8 + z_lo), core: 2. Of those that a mesh axis runs over, the one named last changes fastest.
Arguments:
- positions: float32 [3, 524288], P(None, ('gx', 'gy', 'gz')), may hold values from -1 to 6.5
- charges: float32 [524288], P(('gx', 'gy', 'gz')), may hold values from -1.75 to 1.75
- block_anchor: int32 [3, 4096], P(None, ('gx', 'gy', 'gz')), may hold values from 0 to 120, as said below
- block_atoms: int32 [4096], P(('gx', 'gy', 'gz')), may hold values from 32 to 128, as said below
- brick_blocks: int32 [512], P(('gx', 'gy', 'gz')), may hold values from 4 to 8, as said below
- box_scale: float32 [3], replicated, may hold values from 1.25 to 1.5
Outputs:
- potential: float32 [192, 192, 1024], P('gx', 'gy', 'gz')
- forces: float32 [3, 524288], P(None, ('gx', 'gy', 'gz'))
Inputs may be any that keep to these rules, and one draw needn't show every extreme that they name: `block_anchor`: along x, y, z a block's anchor lies from 0 to 16, 16 and 120 respectively. `block_atoms`: some block is full. `brick_blocks`: some brick uses all 8 block slots.
All inputs are finite; a program needn't handle non-finite values.
Results may differ from a plain program's by a relative error of at most 0.0003.
Values sent between devices are 32-bit elements; how exact they have to be, the bound alone decides.
A program may use at most 64 MiB of HBM per device.

v0:
```python
import math

import jax
import jax.numpy as jnp
from jax import lax
from jax.sharding import PartitionSpec as P

CX = 24
CY = 24
CZ = 128
PATCH = 16
RIM = 4
RADIUS = 4
REACH = 8


SPREAD = 1.0
SMOOTH = 1.5
COUPLING = 200.0


def with_halo(block, sides, width):
    for axis, dim in sides:
        count = lax.axis_size(axis)
        forward = [(i, i + 1) for i in range(count - 1)]
        forward.append((count - 1, 0))
        backward = [(target, source) for source, target in forward]
        low = lax.ppermute(
            lax.slice_in_dim(block, block.shape[dim] - width, None, axis=dim), axis, forward
        )
        high = lax.ppermute(lax.slice_in_dim(block, 0, width, axis=dim), axis, backward)
        block = jnp.concatenate([low, block, high], axis=dim)
    return block


def gaussian(offset, spread_width):
    return jnp.exp(-offset * offset / (2.0 * spread_width * spread_width)) / (
        math.sqrt(2.0 * math.pi) * spread_width
    )


def block_weights(coords, charge_rows, filled, block_index, active_blocks, scale):
    spread_width = SPREAD * scale
    shifted = coords * scale[:, None, None]
    slot_index = jnp.arange(charge_rows.shape[1], dtype=jnp.int32)
    active = (block_index[:, None] < active_blocks) & (slot_index[None, :] < filled[:, None])
    weighted = jnp.where(active, charge_rows, jnp.zeros_like(charge_rows))
    cell_index = jnp.arange(PATCH, dtype=jnp.float32)
    offset_x = shifted[0][:, :, None] + RIM - cell_index
    weight_x = gaussian(offset_x, spread_width[0])
    slope_x = -offset_x / (spread_width[0] * spread_width[0]) * weight_x
    offset_y = shifted[1][:, :, None] + RIM - cell_index
    weight_y = gaussian(offset_y, spread_width[1])
    slope_y = -offset_y / (spread_width[1] * spread_width[1]) * weight_y
    offset_z = shifted[2][:, :, None] + RIM - cell_index
    weight_z = gaussian(offset_z, spread_width[2])
    slope_z = -offset_z / (spread_width[2] * spread_width[2]) * weight_z
    return (weighted, weight_x, slope_x, weight_y, slope_y, weight_z, slope_z)


def spread_patches(weights):
    weighted, weight_x, slope_x, weight_y, slope_y, weight_z, slope_z = weights
    block_count = weighted.shape[0]
    atom_count = weighted.shape[1]
    terms = (
        weighted[:, :, None, None] * weight_x[:, :, :, None] * weight_y[:, :, None, :]
    ).reshape(block_count, atom_count, PATCH * PATCH)
    return jnp.einsum("bsm,bsz->bmz", terms, weight_z, precision=lax.Precision.HIGHEST)


def patch_forces(gathered, weights, scale):
    weighted, weight_x, slope_x, weight_y, slope_y, weight_z, slope_z = weights
    block_count = weighted.shape[0]
    atom_count = weighted.shape[1]
    values_z = jnp.einsum(
        "bmz,bsz->bsm", gathered, weight_z, precision=lax.Precision.HIGHEST
    ).reshape(block_count, atom_count, PATCH, PATCH)
    slopes_z = jnp.einsum(
        "bmz,bsz->bsm", gathered, slope_z, precision=lax.Precision.HIGHEST
    ).reshape(block_count, atom_count, PATCH, PATCH)
    force_x = (
        -weighted
        * scale[0]
        * jnp.einsum(
            "bskl,bsk,bsl->bs", values_z, slope_x, weight_y, precision=lax.Precision.HIGHEST
        )
    )
    force_y = (
        -weighted
        * scale[1]
        * jnp.einsum(
            "bskl,bsk,bsl->bs", values_z, weight_x, slope_y, precision=lax.Precision.HIGHEST
        )
    )
    force_z = (
        -weighted
        * scale[2]
        * jnp.einsum(
            "bskl,bsk,bsl->bs", slopes_z, weight_x, weight_y, precision=lax.Precision.HIGHEST
        )
    )
    return jnp.stack([force_x, force_y, force_z])


def band_matrix(length, scale_axis):
    source = jnp.arange(length, dtype=jnp.int32)[:, None]
    target = jnp.arange(length + 2 * RADIUS, dtype=jnp.int32)[None, :]
    offset = target - RADIUS - source
    kernel = gaussian(offset.astype(jnp.float32), SMOOTH * scale_axis)
    return jnp.where(jnp.abs(offset) <= RADIUS, kernel, jnp.zeros_like(kernel))


def smooth_first(field, scale_axis):
    length, second, third = field.shape
    matrix = band_matrix(length, scale_axis)
    result = jnp.dot(
        matrix.T, field.reshape(length, second * third), precision=lax.Precision.HIGHEST
    )
    return result.reshape(length + 2 * RADIUS, second, third)


def smooth_second(field, scale_axis):
    matrix = band_matrix(field.shape[1], scale_axis)
    return jnp.einsum("xyz,yb->xbz", field, matrix, precision=lax.Precision.HIGHEST)


def smooth_third(field, scale_axis):
    first, second, length = field.shape
    matrix = band_matrix(length, scale_axis)
    result = jnp.dot(field.reshape(first * second, length), matrix, precision=lax.Precision.HIGHEST)
    return result.reshape(first, second, length + 2 * RADIUS)


def edge_pieces(local, axis_dim, owned, rim_width):
    below_rim = lax.slice_in_dim(local, 0, rim_width, axis=axis_dim)
    above_rim = lax.slice_in_dim(
        local, owned + 2 * REACH - rim_width, owned + 2 * REACH, axis=axis_dim
    )
    return jnp.concatenate([below_rim, above_rim], axis=axis_dim)


def fold_edges(local, received, axis_dim, owned, rim_width, margin):
    middle = lax.slice_in_dim(local, REACH - margin, REACH + owned + margin, axis=axis_dim)
    length = owned + 2 * margin
    from_below = lax.slice_in_dim(received, 0, rim_width, axis=axis_dim)
    from_above = lax.slice_in_dim(received, 3 * rim_width, 4 * rim_width, axis=axis_dim)
    pads_below = [(0, 0), (0, 0), (0, 0)]
    pads_below[axis_dim] = (0, length - rim_width)
    pads_above = [(0, 0), (0, 0), (0, 0)]
    pads_above[axis_dim] = (length - rim_width, 0)
    return middle + jnp.pad(from_below, pads_below) + jnp.pad(from_above, pads_above)


def per_device(positions, charges, block_anchor, block_atoms, brick_blocks, box_scale):
    atom_dev = charges.shape[0]
    blocks = block_atoms.shape[0]
    block_len = atom_dev // blocks
    per_step = 4
    group_count = blocks // per_step
    x_cells = CX + 2 * RIM
    y_cells = CY + 2 * RIM
    z_cells = CZ + 2 * RIM
    coords = positions.reshape(3, group_count, per_step, block_len).transpose(1, 0, 2, 3)
    charge_rows = charges.reshape(group_count, per_step, block_len)
    anchors = block_anchor.reshape(3, group_count, per_step).transpose(1, 0, 2)
    filled = block_atoms.reshape(group_count, per_step)
    block_index = jnp.arange(blocks, dtype=jnp.int32).reshape(group_count, per_step)
    active_blocks = brick_blocks[0]
    inputs_all = (coords, charge_rows, anchors, filled, block_index)
    zero_index = jnp.zeros((), jnp.int32)

    def weights_of(inputs_now):
        coords_now, charges_now, anchors_now, filled_now, index_now = inputs_now
        return block_weights(
            coords_now, charges_now, filled_now, index_now, active_blocks, box_scale
        )

    def corner_of(anchors_now, which):
        return (anchors_now[0, which], anchors_now[1, which], anchors_now[2, which])

    def spread_step(density, inputs_now):
        values = spread_patches(weights_of(inputs_now)).reshape(per_step, PATCH, PATCH, PATCH)
        anchors_now = inputs_now[2]
        for which in range(per_step):
            corner = corner_of(anchors_now, which)
            current = lax.dynamic_slice(density, corner, (PATCH, PATCH, PATCH))
            density = lax.dynamic_update_slice(density, current + values[which], corner)
        return (density, None)

    density, _ = lax.scan(
        spread_step, jnp.zeros((x_cells, y_cells, z_cells), jnp.float32), inputs_all
    )
    smoothed = smooth_first(density, box_scale[0])
    smoothed = smooth_second(smoothed, box_scale[1])
    smooth_z = smooth_third(smoothed, box_scale[2])
    rim_width = REACH
    received = with_halo(edge_pieces(smooth_z, 0, CX, rim_width), (("gx", 0),), rim_width)
    settled = fold_edges(smooth_z, received, 0, CX, rim_width, 0)
    received = with_halo(edge_pieces(settled, 1, CY, rim_width), (("gy", 1),), rim_width)
    settled = fold_edges(settled, received, 1, CY, rim_width, 0)
    received = with_halo(edge_pieces(settled, 2, CZ, rim_width), (("gz", 2),), rim_width)
    settled = fold_edges(settled, received, 2, CZ, rim_width, 0)
    potential = COUPLING * settled
    field_wide = with_halo(potential, (("gx", 0), ("gy", 1), ("gz", 2)), RIM)

    def force_step(unused, inputs_now):
        anchors_now = inputs_now[2]
        patches = []
        for which in range(per_step):
            corner = corner_of(anchors_now, which)
            patches.append(lax.dynamic_slice(field_wide, corner, (PATCH, PATCH, PATCH)))
        gathered = jnp.stack(patches).reshape(per_step, PATCH * PATCH, PATCH)
        return (unused, patch_forces(gathered, weights_of(inputs_now), box_scale))

    _, force_groups = lax.scan(force_step, zero_index, inputs_all)
    forces = force_groups.transpose(1, 0, 2, 3).reshape(3, atom_dev)
    return (potential, forces)


def solution(mesh):
    return jax.shard_map(
        per_device,
        mesh=mesh,
        in_specs=(
            P(None, ("gx", "gy", "gz")),
            P(("gx", "gy", "gz")),
            P(None, ("gx", "gy", "gz")),
            P(("gx", "gy", "gz")),
            P(("gx", "gy", "gz")),
            P(),
        ),
        out_specs=(P("gx", "gy", "gz"), P(None, ("gx", "gy", "gz"))),
        check_vma=False,
    )
```

profile of v0, /device:TPU:27, one launch (start us, length us, event | category | flops | bytes accessed | tf_op | source)
XLA Modules:
  0.0 372.4 jit_solution(16478034362604719621)
XLA Ops:
  16.1 75.8 %while.24 = (s32[]{:T(128)}, f32[32,32,136]{1,0,2:T(8,128)S(1)}, s32[2,3,4]{2,1,0:T(4,128)S(1)}, s32[2,4]{1,0:T(2,128)S(1)}, s32[]{:T(128)}, /*index=5*/s32[2,4]...) while((s32[]{:T(128)}, f32[32,32,136]{1,0,2:T(8,128)S(1)}, ...), condition=%wide.region_1.2_spmd, body=%wide.region_0.1_spmd.sunk | while | flops 25448964 | bytes 1872841 | solution.py:190
  44.3 5.2 %dynamic_update_slice.35 = f32[32,32,136]{1,0,2:T(8,128)S(1)} dynamic-update-slice(f32[32,32,136]{1,0,2:T(8,128)S(1)} %dynamic_update_slice.34, f32[16,16,16]{1,0,2:T(8,128)S(1)} %dynamic-slice_add_fusion.11, s32[]{:T(128)S(6)} %select_n.217, s32[]{:T(128)S(6)} %select_n.218, s32[]{:T(128)S(6)} %select_n.219) | dynamic-update-slice | bytes 32772 | tf_op jit(solution)/shard_map/while/body/eval_jaxpr/dynamic_update_slice | solution.py:187
  64.6 5.2 %dynamic_update_slice.33 = f32[32,32,136]{1,0,2:T(8,128)S(1)} dynamic-update-slice(f32[32,32,136]{1,0,2:T(8,128)S(1)} %dynamic_update_slice.32, f32[16,16,16]{1,0,2:T(8,128)S(1)} %dynamic-slice_add_fusion.9, s32[]{:T(128)S(6)} %select_n.211, s32[]{:T(128)S(6)} %select_n.212, s32[]{:T(128)S(6)} %select_n.213) | dynamic-update-slice | bytes 32772 | tf_op jit(solution)/shard_map/while/body/eval_jaxpr/dynamic_update_slice | solution.py:187
  75.6 5.2 %dynamic_update_slice.34 = f32[32,32,136]{1,0,2:T(8,128)S(1)} dynamic-update-slice(f32[32,32,136]{1,0,2:T(8,128)S(1)} %dynamic_update_slice.33, f32[16,16,16]{1,0,2:T(8,128)S(1)} %dynamic-slice_add_fusion.10, s32[]{:T(128)S(6)} %select_n.214, s32[]{:T(128)S(6)} %select_n.215, s32[]{:T(128)S(6)} %select_n.216) | dynamic-update-slice | bytes 32772 | tf_op jit(solution)/shard_map/while/body/eval_jaxpr/dynamic_update_slice | solution.py:187
  86.7 5.2 %dynamic_update_slice.35 = f32[32,32,136]{1,0,2:T(8,128)S(1)} dynamic-update-slice(f32[32,32,136]{1,0,2:T(8,128)S(1)} %dynamic_update_slice.34, f32[16,16,16]{1,0,2:T(8,128)S(1)} %dynamic-slice_add_fusion.11, s32[]{:T(128)S(6)} %select_n.217, s32[]{:T(128)S(6)} %select_n.218, s32[]{:T(128)S(6)} %select_n.219) | dynamic-update-slice | bytes 32772 | tf_op jit(solution)/shard_map/while/body/eval_jaxpr/dynamic_update_slice | solution.py:187
  100.8 10.6 %collective-permute-start = (f32[8,40,144]{2,1,0:T(8,128)S(1)}, f32[8,40,144]{2,1,0:T(8,128)S(1)}, u32[]{:S(2)}, u32[]{:S(2)}) collective-permute-start(f32[8,40,144]{2,1,0:T(8,128)S(1)} %bitcast.269), channel_id=1, source_target_pairs={{0,64},{64,128},{128,192},{192,256},{256,320},{320,384},{384,448},... | collective-permute-start | bytes 552968 | tf_op jit(solution)/shard_map/ppermute | solution.py:28
  112.0 3.3 collective-permute-done
  115.3 2.6 collective-permute-done.1
  118.1 18.2 %collective-permute-start.2 = (f32[24,8,144]{2,1,0:T(8,128)S(1)}, f32[24,8,144]{2,1,0:T(8,128)S(1)}, u32[]{:S(2)}, u32[]{:S(2)}) collective-permute-start(f32[24,8,144]{2,1,0:T(8,128)S(1)} %get-tuple-element.491), channel_id=1, source_target_pairs={{0,8},{8,16},{16,24},{24,32},{32,40},{40,48},{48,56},{56,0},{1,9},... | collective-permute-start | bytes 331784 | tf_op jit(solution)/shard_map/ppermute | solution.py:28
  138.3 13.4 %collective-permute-done.2 = f32[24,8,144]{2,1,0:T(8,128)S(1)} collective-permute-done((f32[24,8,144]{2,1,0:T(8,128)S(1)}, f32[24,8,144]{2,1,0:T(8,128)S(1)}, u32[]{:S(2)}, u32[]{:S(2)}) %collective-permute-start.2) | collective-permute-done | bytes 110624 | tf_op jit(solution)/shard_map/ppermute | solution.py:28
  151.7 15.0 %collective-permute-done.3 = f32[24,8,144]{2,1,0:T(8,128)S(1)} collective-permute-done((f32[24,8,144]{2,1,0:T(8,128)S(1)}, f32[24,8,144]{2,1,0:T(8,128)S(1)}, u32[]{:S(2)}, u32[]{:S(2)}) %collective-permute-start.3) | collective-permute-done | bytes 110624 | tf_op jit(solution)/shard_map/ppermute | solution.py:31
  168.9 10.0 %collective-permute-start.5 = (f32[24,24,8]{2,1,0:T(8,128)S(1)}, f32[24,24,8]{2,1,0:T(8,128)S(1)}, u32[]{:S(2)}, u32[]{:S(2)}) collective-permute-start(f32[24,24,8]{2,1,0:T(8,128)S(1)} %get-tuple-element.496), channel_id=1, source_target_pairs={{1,0},{2,1},{3,2},{4,3},{5,4},{6,5},{7,6},{0,7},{9,8},{10,9},{11,1... | collective-permute-start | bytes 55304 | tf_op jit(solution)/shard_map/ppermute | solution.py:31
  178.9 4.3 %collective-permute-done.4 = f32[24,24,8]{2,1,0:T(8,128)S(1)} collective-permute-done((f32[24,24,8]{2,1,0:T(8,128)S(1)}, f32[24,24,8]{2,1,0:T(8,128)S(1)}, u32[]{:S(2)}, u32[]{:S(2)}) %collective-permute-start.4) | collective-permute-done | bytes 18464 | tf_op jit(solution)/shard_map/ppermute | solution.py:28
  184.3 8.6 %collective-permute-start.6 = (f32[4,24,128]{2,1,0:T(8,128)S(1)}, f32[4,24,128]{2,1,0:T(8,128)S(1)}, u32[]{:S(2)}, u32[]{:S(2)}) collective-permute-start(f32[4,24,128]{2,1,0:T(8,128)S(1)} %get-tuple-element.501), channel_id=1, source_target_pairs={{0,64},{64,128},{128,192},{192,256},{256,320},{320,384},{384,448},... | collective-permute-start | bytes 147464 | tf_op jit(solution)/shard_map/ppermute | solution.py:28
  198.4 3.4 collective-permute-start.9
  201.8 12.6 %collective-permute-done.9 = f32[32,4,128]{2,1,0:T(4,128)S(1)} collective-permute-done((f32[32,4,128]{2,1,0:T(4,128)S(1)}, f32[32,4,128]{2,1,0:T(4,128)S(1)}, u32[]{:S(2)}, u32[]{:S(2)}) %collective-permute-start.9) | collective-permute-done | bytes 65568 | tf_op jit(solution)/shard_map/ppermute | solution.py:31
  217.0 9.5 %collective-permute-start.11 = (f32[32,32,4]{2,1,0:T(8,128)S(1)}, f32[32,32,4]{2,1,0:T(8,128)S(1)}, u32[]{:S(2)}, u32[]{:S(2)}) collective-permute-start(f32[32,32,4]{2,1,0:T(8,128)S(1)} %get-tuple-element.498), channel_id=1, source_target_pairs={{1,0},{2,1},{3,2},{4,3},{5,4},{6,5},{7,6},{0,7},{9,8},{10,9},{11,1... | collective-permute-start | bytes 49160 | tf_op jit(solution)/shard_map/ppermute | solution.py:31
  226.6 10.2 %collective-permute-done.10 = f32[32,32,4]{2,1,0:T(8,128)S(1)} collective-permute-done((f32[32,32,4]{2,1,0:T(8,128)S(1)}, f32[32,32,4]{2,1,0:T(8,128)S(1)}, u32[]{:S(2)}, u32[]{:S(2)}) %collective-permute-start.10) | collective-permute-done | bytes 16416 | tf_op jit(solution)/shard_map/ppermute | solution.py:28
  236.8 7.1 %collective-permute-done.11 = f32[32,32,4]{2,1,0:T(8,128)S(1)} collective-permute-done((f32[32,32,4]{2,1,0:T(8,128)S(1)}, f32[32,32,4]{2,1,0:T(8,128)S(1)}, u32[]{:S(2)}, u32[]{:S(2)}) %collective-permute-start.11) | collective-permute-done | bytes 16416 | tf_op jit(solution)/shard_map/ppermute | solution.py:31
  247.9 123.1 %while.25 = (s32[]{:T(128)}, f32[2,3,4,128]{3,2,1,0:T(4,128)}, s32[2,4]{1,0:T(2,128)}, s32[]{:T(128)}, s32[2,4]{1,0:T(2,128)}, /*index=5*/f32[2,4,128]{2,1,0:T(4...) while((s32[]{:T(128)}, f32[2,3,4,128]{3,2,1,0:T(4,128)}, ...), condition=%wide.region_3.4_spmd, body=%wide.region_2.3_spmd.sunk | while | flops 55322152 | bytes 8399301 | solution.py:215
  273.6 2.9 copy.59
  276.6 8.4 %fusion.177 = f32[4,128,1,16]{3,2,1,0:T(1,128)S(1)} fusion(f32[4,128,16,16]{2,3,1,0:T(8,128)} %copy.59, f32[4,128,16,1]{2,3,1,0:T(1,128)S(1)} %bitcast.257), kind=kOutput, calls=%fused_computation.168.clone.1 | convolution fusion | flops 1572864 | bytes 589824 | tf_op jit(solution)/shard_map/while/body/eval_jaxpr/bskl,bsk,bsl->bs/dot_general | solution.py:98
  286.1 2.9 copy.58
  289.0 8.6 %fusion.175 = f32[4,128,1,16]{3,2,1,0:T(1,128)S(1)} fusion(f32[4,128,16,16]{2,3,1,0:T(8,128)} %copy.58, f32[4,128,16,1]{2,3,1,0:T(1,128)S(1)} %bitcast.258), kind=kOutput, calls=%fused_computation.167.clone.1 | convolution fusion | flops 1572864 | bytes 589824 | tf_op jit(solution)/shard_map/while/body/eval_jaxpr/bskl,bsk,bsl->bs/dot_general | solution.py:91
  297.7 6.8 %fusion.174 = f32[4,128,1,16]{3,2,1,0:T(1,128)S(1)} fusion(f32[4,128,16,16]{2,3,1,0:T(8,128)S(1)} %copy-done, f32[4,128,16,1]{2,3,1,0:T(1,128)S(1)} %bitcast.262), kind=kOutput, calls=%fused_computation.166.clone.1 | convolution fusion | flops 1572864 | bytes 589824 | tf_op jit(solution)/shard_map/while/body/eval_jaxpr/bskl,bsk,bsl->bs/dot_general | solution.py:84
  306.3 2.7 multiply_bitcast_fusion.4
  335.0 2.9 copy.59
  338.1 8.4 %fusion.177 = f32[4,128,1,16]{3,2,1,0:T(1,128)S(1)} fusion(f32[4,128,16,16]{2,3,1,0:T(8,128)} %copy.59, f32[4,128,16,1]{2,3,1,0:T(1,128)S(1)} %bitcast.257), kind=kOutput, calls=%fused_computation.168.clone.1 | convolution fusion | flops 1572864 | bytes 589824 | tf_op jit(solution)/shard_map/while/body/eval_jaxpr/bskl,bsk,bsl->bs/dot_general | solution.py:98
  347.6 2.9 copy.58
  350.5 8.6 %fusion.175 = f32[4,128,1,16]{3,2,1,0:T(1,128)S(1)} fusion(f32[4,128,16,16]{2,3,1,0:T(8,128)} %copy.58, f32[4,128,16,1]{2,3,1,0:T(1,128)S(1)} %bitcast.258), kind=kOutput, calls=%fused_computation.167.clone.1 | convolution fusion | flops 1572864 | bytes 589824 | tf_op jit(solution)/shard_map/while/body/eval_jaxpr/bskl,bsk,bsl->bs/dot_general | solution.py:91
  359.1 6.8 %fusion.174 = f32[4,128,1,16]{3,2,1,0:T(1,128)S(1)} fusion(f32[4,128,16,16]{2,3,1,0:T(8,128)S(1)} %copy-done, f32[4,128,16,1]{2,3,1,0:T(1,128)S(1)} %bitcast.262), kind=kOutput, calls=%fused_computation.166.clone.1 | convolution fusion | flops 1572864 | bytes 589824 | tf_op jit(solution)/shard_map/while/body/eval_jaxpr/bskl,bsk,bsl->bs/dot_general | solution.py:84
  367.7 2.7 multiply_bitcast_fusion.4
  (185 shorter events, 55.9 us)
Async XLA Ops:
  0.6 15.4 %copy-start.4 = (f32[3]{0:T(128)S(1)}, f32[3]{0:T(128)}, u32[]{:S(2)}) copy-start(f32[3]{0:T(128)} %param.15) | copy-start | bytes 40
  91.9 8.7 %copy-start.10 = (s32[2,4]{1,0:T(2,128)}, s32[2,4]{1,0:T(2,128)S(1)}, u32[]{:S(2)}) copy-start(s32[2,4]{1,0:T(2,128)S(1)} %get-tuple-element.968) | copy-start | bytes 100
  100.8 14.6 %collective-permute-start = (f32[8,40,144]{2,1,0:T(8,128)S(1)}, f32[8,40,144]{2,1,0:T(8,128)S(1)}, u32[]{:S(2)}, u32[]{:S(2)}) collective-permute-start(f32[8,40,144]{2,1,0:T(8,128)S(1)} %bitcast.269), channel_id=1, source_target_pairs={{0,64},{64,128},{128,192},{192,256},{256,320},{320,384},{384,448},... | collective-permute-start | bytes 552968 | tf_op jit(solution)/shard_map/ppermute | solution.py:28
  111.5 6.5 %collective-permute-start.1 = (f32[8,40,144]{2,1,0:T(8,128)S(1)}, f32[8,40,144]{2,1,0:T(8,128)S(1)}, u32[]{:S(2)}, u32[]{:S(2)}) collective-permute-start(f32[8,40,144]{2,1,0:T(8,128)S(1)} %bitcast.270), channel_id=1, source_target_pairs={{64,0},{128,64},{192,128},{256,192},{320,256},{384,320},{448,384},... | collective-permute-start | bytes 552968 | tf_op jit(solution)/shard_map/ppermute | solution.py:31
  118.1 33.6 %collective-permute-start.2 = (f32[24,8,144]{2,1,0:T(8,128)S(1)}, f32[24,8,144]{2,1,0:T(8,128)S(1)}, u32[]{:S(2)}, u32[]{:S(2)}) collective-permute-start(f32[24,8,144]{2,1,0:T(8,128)S(1)} %get-tuple-element.491), channel_id=1, source_target_pairs={{0,8},{8,16},{16,24},{24,32},{32,40},{40,48},{48,56},{56,0},{1,9},... | collective-permute-start | bytes 331784 | tf_op jit(solution)/shard_map/ppermute | solution.py:28
  136.4 30.4 %collective-permute-start.3 = (f32[24,8,144]{2,1,0:T(8,128)S(1)}, f32[24,8,144]{2,1,0:T(8,128)S(1)}, u32[]{:S(2)}, u32[]{:S(2)}) collective-permute-start(f32[24,8,144]{2,1,0:T(8,128)S(1)} %get-tuple-element.492), channel_id=1, source_target_pairs={{8,0},{16,8},{24,16},{32,24},{40,32},{48,40},{56,48},{0,56},{9,1},... | collective-permute-start | bytes 331784 | tf_op jit(solution)/shard_map/ppermute | solution.py:31
  167.0 16.2 %collective-permute-start.4 = (f32[24,24,8]{2,1,0:T(8,128)S(1)}, f32[24,24,8]{2,1,0:T(8,128)S(1)}, u32[]{:S(2)}, u32[]{:S(2)}) collective-permute-start(f32[24,24,8]{2,1,0:T(8,128)S(1)} %get-tuple-element.495), channel_id=1, source_target_pairs={{0,1},{1,2},{2,3},{3,4},{4,5},{5,6},{6,7},{7,0},{8,9},{9,10},{10,1... | collective-permute-start | bytes 55304 | tf_op jit(solution)/shard_map/ppermute | solution.py:28
  168.9 15.2 %collective-permute-start.5 = (f32[24,24,8]{2,1,0:T(8,128)S(1)}, f32[24,24,8]{2,1,0:T(8,128)S(1)}, u32[]{:S(2)}, u32[]{:S(2)}) collective-permute-start(f32[24,24,8]{2,1,0:T(8,128)S(1)} %get-tuple-element.496), channel_id=1, source_target_pairs={{1,0},{2,1},{3,2},{4,3},{5,4},{6,5},{7,6},{0,7},{9,8},{10,9},{11,1... | collective-permute-start | bytes 55304 | tf_op jit(solution)/shard_map/ppermute | solution.py:31
  184.3 61.2 %copy-start.3 = (f32[24,24,128]{2,1,0:T(8,128)}, f32[24,24,128]{2,1,0:T(8,128)S(1)}, u32[]{:S(2)}) copy-start(f32[24,24,128]{2,1,0:T(8,128)S(1)} %fusion.56) | copy-start | bytes 884740
  184.3 9.8 %collective-permute-start.6 = (f32[4,24,128]{2,1,0:T(8,128)S(1)}, f32[4,24,128]{2,1,0:T(8,128)S(1)}, u32[]{:S(2)}, u32[]{:S(2)}) collective-permute-start(f32[4,24,128]{2,1,0:T(8,128)S(1)} %get-tuple-element.501), channel_id=1, source_target_pairs={{0,64},{64,128},{128,192},{192,256},{256,320},{320,384},{384,448},... | collective-permute-start | bytes 147464 | tf_op jit(solution)/shard_map/ppermute | solution.py:28
  192.9 3.5 collective-permute-start.7
  196.5 5.3 %collective-permute-start.8 = (f32[32,4,128]{2,1,0:T(4,128)S(1)}, f32[32,4,128]{2,1,0:T(4,128)S(1)}, u32[]{:S(2)}, u32[]{:S(2)}) collective-permute-start(f32[32,4,128]{2,1,0:T(4,128)S(1)} %get-tuple-element.499), channel_id=1, source_target_pairs={{0,8},{8,16},{16,24},{24,32},{32,40},{40,48},{48,56},{56,0},{1,9},... | collective-permute-start | bytes 196616 | tf_op jit(solution)/shard_map/ppermute | solution.py:28
  198.4 16.0 %collective-permute-start.9 = (f32[32,4,128]{2,1,0:T(4,128)S(1)}, f32[32,4,128]{2,1,0:T(4,128)S(1)}, u32[]{:S(2)}, u32[]{:S(2)}) collective-permute-start(f32[32,4,128]{2,1,0:T(4,128)S(1)} %get-tuple-element.500), channel_id=1, source_target_pairs={{8,0},{16,8},{24,16},{32,24},{40,32},{48,40},{56,48},{0,56},{9,1},... | collective-permute-start | bytes 196616 | tf_op jit(solution)/shard_map/ppermute | solution.py:31
  214.7 22.1 %collective-permute-start.10 = (f32[32,32,4]{2,1,0:T(8,128)S(1)}, f32[32,32,4]{2,1,0:T(8,128)S(1)}, u32[]{:S(2)}, u32[]{:S(2)}) collective-permute-start(f32[32,32,4]{2,1,0:T(8,128)S(1)} %get-tuple-element.497), channel_id=1, source_target_pairs={{0,1},{1,2},{2,3},{3,4},{4,5},{5,6},{6,7},{7,0},{8,9},{9,10},{10,1... | collective-permute-start | bytes 49160 | tf_op jit(solution)/shard_map/ppermute | solution.py:28
  217.0 26.9 %collective-permute-start.11 = (f32[32,32,4]{2,1,0:T(8,128)S(1)}, f32[32,32,4]{2,1,0:T(8,128)S(1)}, u32[]{:S(2)}, u32[]{:S(2)}) collective-permute-start(f32[32,32,4]{2,1,0:T(8,128)S(1)} %get-tuple-element.498), channel_id=1, source_target_pairs={{1,0},{2,1},{3,2},{4,3},{5,4},{6,5},{7,6},{0,7},{9,8},{10,9},{11,1... | collective-permute-start | bytes 49160 | tf_op jit(solution)/shard_map/ppermute | solution.py:31
  248.1 28.3 %copy-start.5 = (f32[3]{0:T(128)}, f32[3]{0:T(128)S(1)}, u32[]{:S(2)}) copy-start(f32[3]{0:T(128)S(1)} %get-tuple-element.923) | copy-start | bytes 40 | tf_op jit(solution)/shard_map/while
  248.1 28.3 %copy-start.8 = (s32[2,3,4]{2,1,0:T(4,128)}, s32[2,3,4]{2,1,0:T(4,128)S(1)}, u32[]{:S(2)}) copy-start(s32[2,3,4]{2,1,0:T(4,128)S(1)} %get-tuple-element.929) | copy-start | bytes 292 | tf_op jit(solution)/shard_map/while
  276.6 8.4 %copy-start.2 = (f32[4,256,16]{1,2,0:T(8,128)S(1)}, f32[4,256,16]{1,2,0:T(8,128)}, u32[]{:S(2)}) copy-start(f32[4,256,16]{1,2,0:T(8,128)} %copy-done.1) | copy-start | bytes 196612 | tf_op jit(solution)/shard_map/while
  289.0 8.6 %copy-start = (f32[4,128,16,16]{2,3,1,0:T(8,128)S(1)}, f32[4,128,16,16]{2,3,1,0:T(8,128)}, u32[]{:S(2)}) copy-start(f32[4,128,16,16]{2,3,1,0:T(8,128)} %copy.58) | copy-start | bytes 1572868 | tf_op jit(solution)/shard_map/while
  297.7 7.9 %copy-start.15 = (s32[2,4]{1,0:T(2,128)S(1)}, s32[2,4]{1,0:T(2,128)}, u32[]{:S(2)}) copy-start(s32[2,4]{1,0:T(2,128)} %get-tuple-element.921) | copy-start | bytes 100 | tf_op jit(solution)/shard_map/while
  297.7 7.9 %copy-start.6 = (f32[3]{0:T(128)S(1)}, f32[3]{0:T(128)}, u32[]{:S(2)}) copy-start(f32[3]{0:T(128)} %copy-done.5) | copy-start | bytes 40 | tf_op jit(solution)/shard_map/while
  297.7 11.3 %copy-start.12 = (f32[2,3,4,128]{3,2,1,0:T(4,128)S(1)}, f32[2,3,4,128]{3,2,1,0:T(4,128)}, u32[]{:S(2)}) copy-start(f32[2,3,4,128]{3,2,1,0:T(4,128)} %get-tuple-element.895) | copy-start | bytes 36868 | tf_op jit(solution)/shard_map/while
  297.7 11.9 %copy-start.9 = (s32[2,3,4]{2,1,0:T(4,128)S(1)}, s32[2,3,4]{2,1,0:T(4,128)}, u32[]{:S(2)}) copy-start(s32[2,3,4]{2,1,0:T(4,128)} %copy-done.8) | copy-start | bytes 292 | tf_op jit(solution)/shard_map/while
  309.6 28.3 %copy-start.5 = (f32[3]{0:T(128)}, f32[3]{0:T(128)S(1)}, u32[]{:S(2)}) copy-start(f32[3]{0:T(128)S(1)} %get-tuple-element.923) | copy-start | bytes 40 | tf_op jit(solution)/shard_map/while
  309.6 28.3 %copy-start.8 = (s32[2,3,4]{2,1,0:T(4,128)}, s32[2,3,4]{2,1,0:T(4,128)S(1)}, u32[]{:S(2)}) copy-start(s32[2,3,4]{2,1,0:T(4,128)S(1)} %get-tuple-element.929) | copy-start | bytes 292 | tf_op jit(solution)/shard_map/while
  338.1 8.4 %copy-start.2 = (f32[4,256,16]{1,2,0:T(8,128)S(1)}, f32[4,256,16]{1,2,0:T(8,128)}, u32[]{:S(2)}) copy-start(f32[4,256,16]{1,2,0:T(8,128)} %copy-done.1) | copy-start | bytes 196612 | tf_op jit(solution)/shard_map/while
  350.4 8.6 %copy-start = (f32[4,128,16,16]{2,3,1,0:T(8,128)S(1)}, f32[4,128,16,16]{2,3,1,0:T(8,128)}, u32[]{:S(2)}) copy-start(f32[4,128,16,16]{2,3,1,0:T(8,128)} %copy.58) | copy-start | bytes 1572868 | tf_op jit(solution)/shard_map/while
  359.1 7.3 %copy-start.11 = (s32[2,4]{1,0:T(2,128)S(1)}, s32[2,4]{1,0:T(2,128)}, u32[]{:S(2)}) copy-start(s32[2,4]{1,0:T(2,128)} %get-tuple-element.919) | copy-start | bytes 100 | tf_op jit(solution)/shard_map/while
  359.1 7.9 %copy-start.15 = (s32[2,4]{1,0:T(2,128)S(1)}, s32[2,4]{1,0:T(2,128)}, u32[]{:S(2)}) copy-start(s32[2,4]{1,0:T(2,128)} %get-tuple-element.921) | copy-start | bytes 100 | tf_op jit(solution)/shard_map/while
  359.1 7.9 %copy-start.6 = (f32[3]{0:T(128)S(1)}, f32[3]{0:T(128)}, u32[]{:S(2)}) copy-start(f32[3]{0:T(128)} %copy-done.5) | copy-start | bytes 40 | tf_op jit(solution)/shard_map/while
  359.1 11.3 %copy-start.12 = (f32[2,3,4,128]{3,2,1,0:T(4,128)S(1)}, f32[2,3,4,128]{3,2,1,0:T(4,128)}, u32[]{:S(2)}) copy-start(f32[2,3,4,128]{3,2,1,0:T(4,128)} %get-tuple-element.895) | copy-start | bytes 36868 | tf_op jit(solution)/shard_map/while
  359.1 11.9 %copy-start.9 = (s32[2,3,4]{2,1,0:T(4,128)S(1)}, s32[2,3,4]{2,1,0:T(4,128)}, u32[]{:S(2)}) copy-start(s32[2,3,4]{2,1,0:T(4,128)} %copy-done.8) | copy-start | bytes 292 | tf_op jit(solution)/shard_map/while
  (8 other events, 33.3 us)
where the time goes:
time: 373 us; the launch traced here: 372 us
  loops' own time  89.8 us (24%)
  waiting for transfers between devices  73.1 us (20%)
  starting transfers between devices  68.4 us (18%)
  matrix products  58.3 us (16%)
  local copies, waits for them, and re-layouts  55 us (15%)
  other arithmetic  15.4 us (4%)
  between operations  12.4 us (3%)
    another operation x1, loops' own time, per_device(): _, force_groups = lax.scan(force_step, zero_index, inputs_all)  45.2 us
    another operation x1, loops' own time, per_device(): lax.scan(spread_step, jnp.zeros((x_cells, y_cells, z_cells), jnp.float32)...  44.6 us
    ppermute x6, starting transfers between devices, with_halo(): lax.ppermute(lax.slice_in_dim(block, block.shape[dim] - width, None, axis...  43.6 us
    ppermute x6, waiting for transfers between devices, with_halo(): lax.ppermute(lax.slice_in_dim(block, 0, width, axis=dim), axis, backward)  40.6 us
    ppermute x6, waiting for transfers between devices, with_halo(): lax.ppermute(lax.slice_in_dim(block, block.shape[dim] - width, None, axis...  32.4 us
    ppermute x6, starting transfers between devices, with_halo(): lax.ppermute(lax.slice_in_dim(block, 0, width, axis=dim), axis, backward)  24.8 us
    dynamic_update_slice x8, local copies, waits for them, and re-layouts, spread_step(): density = lax.dynamic_update_slice(density, current + values[which], corner)  23.9 us
    dot_general x2, matrix products, patch_forces(): jnp.einsum('bskl,bsk,bsl->bs', values_z, weight_x, slope_y, precision=lax...  17.2 us
  transfers between devices with their start and end apart: 12, of which 11 were waited for; matrix products, arithmetic and copies ran while one was open for 0% of the time, Pallas kernels for 0%

commit v1 on v0

v1 whole, which is shorter than its diff:
```python
import math
import jax, jax.numpy as jnp
from jax import lax
from jax.experimental import pallas as pl
from jax.experimental.pallas import tpu as pltpu

from jax.sharding import PartitionSpec as P

MESH = pl.DeviceIdType.MESH
CX = 24
CY = 24
CZ = 128
PATCH = 16
RIM = 4
RADIUS = 4
SPREAD = 1.0
SMOOTH = 1.5
COUPLING = 200.0
ROWS = 40
BLOCKS = 8
LANES = 128
SOURCES = 27
SLOTS = SOURCES * BLOCKS
SPAN = 32
Z_ROWS = 176
WAYS = 4
PAD = 40


def norm(width):
    return 1.0 / (math.sqrt(2.0 * math.pi) * width)


def window(coord, place, width):
    offset = coord + RIM - place.astype(jnp.float32)
    inside = (place >= 0) & (place < PATCH)
    weight = jnp.exp(-offset * offset / (2.0 * width * width)) * norm(width)
    weight = jnp.where(inside, weight, 0.0)
    return weight, -offset / (width * width) * weight


def split(value):
    high = value.astype(jnp.bfloat16)
    return high, (value - high.astype(jnp.float32)).astype(jnp.bfloat16)


def field_kernel(meta, scale_ref, atoms, potential, forces, order, tasks, starts, pad_x, pad_y, pad_z, wx_all, wy_all, wz_all, density, field):
    f32 = jnp.float32
    scales = [jnp.full((1, LANES), scale_ref[a], f32) for a in range(3)]
    widths = [SPREAD * s for s in scales]
    taps = []
    for a in range(3):
        tau = SMOOTH * scales[a]
        taps.append([jnp.exp(-float(e * e) / (2.0 * tau * tau)) * norm(tau) for e in range(RADIUS + 1)])
    density[...] = jnp.zeros_like(density)
    for ref in (pad_x, pad_y, pad_z):
        ref[...] = jnp.zeros_like(ref)
    wx_all[pl.ds(SLOTS * SPAN, SPAN), :] = jnp.zeros((SPAN, LANES), f32)
    wy_all[pl.ds(SLOTS * SPAN, SPAN), :] = jnp.zeros((SPAN, LANES), f32)
    wz_all[pl.ds(SLOTS * 24, 24), :] = jnp.zeros((24, LANES), f32)
    starts[SLOTS] = 0

    def choose(n, count):
        cx = n // 9
        cz = n // 3 % 3
        cy = n % 3
        low_x = jnp.where(cx == 1, 5, 0)
        high_x = jnp.where(cx == 2, 11, 999)
        low_y = jnp.where(cy == 1, 5, 0)
        high_y = jnp.where(cy == 2, 11, 999)
        low_z = jnp.where(cz == 1, CZ - 19, 0)
        high_z = jnp.where(cz == 2, 11, 999)
        for b in range(BLOCKS):
            x = meta[n, b]
            y = meta[n, BLOCKS + b]
            z = meta[n, 2 * BLOCKS + b]
            live = meta[n, 3 * BLOCKS + b]
            near = (x >= low_x) & (x <= high_x) & (y >= low_y) & (y <= high_y) & (z >= low_z) & (z <= high_z) & (live > 0)
            order[count] = n * BLOCKS + b
            count = count + near.astype(jnp.int32)
        return count

    blocks = lax.fori_loop(0, SOURCES, choose, jnp.int32(0))
    for extra in range(WAYS - 1):
        order[blocks + extra] = 0

    iota16 = lax.broadcasted_iota(jnp.int32, (PATCH, LANES), 0)

    def weigh(group, count):
        for way in range(WAYS):
            k = group * WAYS + way
            code = order[k]
            n = code // BLOCKS
            b = code % BLOCKS
            cx = n // 9
            cz = n // 3 % 3
            cy = n % 3
            off_x = meta[n, b] + jnp.where(cx == 0, 0, jnp.where(cx == 1, -CX, CX))
            off_y = meta[n, BLOCKS + b] + jnp.where(cy == 0, 0, jnp.where(cy == 1, -CY, CY))
            off_z = meta[n, 2 * BLOCKS + b] + jnp.where(cz == 0, 0, jnp.where(cz == 1, -CZ, CZ))
            row = n * ROWS + b
            x = atoms[pl.ds(row, 1), :] * scales[0]
            y = atoms[pl.ds(row + BLOCKS, 1), :] * scales[1]
            z = atoms[pl.ds(row + 2 * BLOCKS, 1), :] * scales[2]
            q = atoms[pl.ds(row + 3 * BLOCKS, 1), :]
            pad_x[way, pl.ds(PAD, PATCH), :] = q * window(x, iota16, widths[0])[0]
            pad_y[way, pl.ds(PAD, PATCH), :] = window(y, iota16, widths[1])[0]
            pad_z[way, pl.ds(8, PATCH), :] = window(z, iota16, widths[2])[0]
            for a, off, pad, out in ((0, off_x, pad_x, wx_all), (1, off_y, pad_y, wy_all)):
                start = PAD - off
                total = taps[a][0] * pad[way, pl.ds(start, SPAN), :]
                for e in range(1, RADIUS + 1):
                    total = total + taps[a][e] * (pad[way, pl.ds(start - e, SPAN), :] + pad[way, pl.ds(start + e, SPAN), :])
                out[pl.ds(pl.multiple_of(k * SPAN, SPAN), SPAN), :] = total
            first = off_z + 20
            shift = first % 8
            wz_all[pl.ds(pl.multiple_of(k * 24, 8), 24), :] = pad_z[way, pl.ds(8 - shift, 24), :]
            starts[k] = first - shift
            used = k < blocks
            for half in range(2):
                for side in range(2):
                    touches = used & ((cx == 0) | (cx == half + 1)) & ((cy == 0) | (cy == side + 1))
                    tasks[count] = k * 4 + half * 2 + side
                    count = count + touches.astype(jnp.int32)
        return count

    jobs = lax.fori_loop(0, (blocks + WAYS - 1) // WAYS, weigh, jnp.int32(0))
    for extra in range(WAYS - 1):
        tasks[jobs + extra] = SLOTS * 4

    def spread(group, carry):
        for way in range(WAYS):
            code = tasks[group * WAYS + way]
            k = code // 4
            half = code // 2 % 2
            side = code % 2
            wx = wx_all[pl.ds(pl.multiple_of(k * SPAN + half * 16, 16), 16), :]
            wy = wy_all[pl.ds(pl.multiple_of(k * SPAN + side * 16, 16), 16), :]
            product = (wx[:, None, :] * wy[None, :, :]).reshape(256, LANES)
            high, low = split(product)
            wz = wz_all[pl.ds(pl.multiple_of(k * 24, 8), 24), :]
            z_high = wz.astype(jnp.bfloat16).astype(f32)
            left = jnp.concatenate([z_high, wz - z_high], axis=0).astype(jnp.bfloat16)
            patch = lax.dot_general(
                jnp.concatenate([left, left], axis=1), jnp.concatenate([high, low], axis=1),
                (((1,), (1,)), ((), ())), preferred_element_type=f32)
            rows = pl.ds(pl.multiple_of((code % 4) * Z_ROWS + starts[k], 8), 24)
            density[rows, :] = density[rows, :] + patch[:24] + patch[24:]
        return carry

    lax.fori_loop(0, (jobs + WAYS - 1) // WAYS, spread, jnp.int32(0))

    length = CZ + 2 * (RIM + RADIUS)
    gap = lax.broadcasted_iota(jnp.int32, (length, length), 0) - lax.broadcasted_iota(jnp.int32, (length, length), 1)
    tau = SMOOTH * scale_ref[2]
    gap_f = gap.astype(f32)
    tau_v = jnp.full((length, length), tau, f32)
    band = jnp.exp(-gap_f * gap_f / (2.0 * tau_v * tau_v)) * (COUPLING / (math.sqrt(2.0 * math.pi) * tau_v))
    band_high, band_low = split(jnp.where(jnp.abs(gap) <= RADIUS, band, 0.0))
    for half in range(2):
        for side in range(2):
            part = density[pl.ds((half * 2 + side) * Z_ROWS + 16, length), :]
            high, low = split(part)
            smooth = (jnp.dot(band_high, high, preferred_element_type=f32)
                      + jnp.dot(band_high, low, preferred_element_type=f32)
                      + jnp.dot(band_low, high, preferred_element_type=f32))
            turned = smooth[8:8 + CZ].T
            edge = jnp.concatenate([smooth[4:8], smooth[8 + CZ:12 + CZ]], axis=0)
            edge_high = edge.astype(jnp.bfloat16).astype(f32)
            edges = jnp.concatenate([edge_high, edge - edge_high, edge_high, jnp.zeros((LANES - 24, 256), f32)], axis=0).T
            turned_high, turned_low = split(turned)
            cube = turned.reshape(16, 16, CZ)
            low_x, low_y = (1 - half) * RIM, (1 - side) * RIM
            potential[pl.ds(half * 12, 12), pl.ds(side * 12, 12), :] = cube[low_x:low_x + 12, low_y:low_y + 12, :]
            place = (pl.ds(half * 16, 16), pl.ds(side * 16, 16))
            for i, block in enumerate((turned_high, turned_low, turned_high, edges.astype(jnp.bfloat16))):
                field[place[0], place[1], pl.ds(i * LANES, LANES)] = block.reshape(16, 16, LANES)

    iota32 = lax.broadcasted_iota(jnp.int32, (SPAN, LANES), 0)
    iota_z = lax.broadcasted_iota(jnp.int32, (CZ, LANES), 0)
    iota8 = lax.broadcasted_iota(jnp.int32, (8, LANES), 0)
    edge_z = jnp.where(iota8 < 4, iota8 - 4, iota8 + (CZ - 4))

    def force(b):
        x = atoms[pl.ds(b, 1), :] * scales[0]
        y = atoms[pl.ds(b + BLOCKS, 1), :] * scales[1]
        z = atoms[pl.ds(b + 2 * BLOCKS, 1), :] * scales[2]
        q = atoms[pl.ds(b + 3 * BLOCKS, 1), :]
        at_x = meta[0, b]
        at_y = meta[0, BLOCKS + b]
        at_z = meta[0, 2 * BLOCKS + b]
        wx, sx = window(x, iota16, widths[0])
        wy, sy = window(y, iota32 - at_y, widths[1])
        wz, sz = window(z, iota_z - at_z + RIM, widths[2])
        we, se = window(z, edge_z - at_z + RIM, widths[2])
        main_high, main_low = split(jnp.concatenate([wz, sz], axis=1))
        rim = jnp.concatenate([we, se], axis=1)
        rim_high = rim.astype(jnp.bfloat16).astype(f32)
        rim = jnp.concatenate([rim_high, rim_high, rim - rim_high, jnp.zeros((LANES - 24, 256), f32)], axis=0).astype(jnp.bfloat16)
        right = jnp.concatenate([main_high, main_high, main_low, rim], axis=0)
        left = field[pl.ds(at_x, PATCH)].reshape(PATCH * SPAN, 4 * LANES)
        values = jnp.dot(left, right, preferred_element_type=f32).reshape(PATCH, SPAN, 256)
        by_sx = jnp.zeros((SPAN, LANES), f32)
        by_wx = jnp.zeros((SPAN, LANES), f32)
        by_wz = jnp.zeros((SPAN, LANES), f32)
        for i in range(PATCH):
            level = values[i, :, :LANES]
            by_sx = by_sx + level * sx[i:i + 1]
            by_wx = by_wx + level * wx[i:i + 1]
            by_wz = by_wz + values[i, :, LANES:] * wx[i:i + 1]
        for a, total in enumerate((by_sx * wy, by_wx * sy, by_wz * wy)):
            forces[a:a + 1, b * LANES:(b + 1) * LANES] = -q * scales[a] * jnp.sum(total, axis=0, keepdims=True)

    for b in range(BLOCKS):
        force(b)


def make_field(atoms, meta, box_scale):
    smem = pl.BlockSpec(memory_space=pltpu.SMEM)
    vmem = pl.BlockSpec(memory_space=pltpu.VMEM)
    f32 = jnp.float32
    return pl.pallas_call(
        field_kernel,
        out_shape=(jax.ShapeDtypeStruct((CX, CY, CZ), f32), jax.ShapeDtypeStruct((3, BLOCKS * LANES), f32)),
        in_specs=[smem, smem, vmem],
        out_specs=(vmem, vmem),
        scratch_shapes=[
            pltpu.SMEM((SLOTS + 8,), jnp.int32),
            pltpu.SMEM((SLOTS * 4 + 8,), jnp.int32),
            pltpu.SMEM((SLOTS + 8,), jnp.int32),
            pltpu.VMEM((WAYS, 96, LANES), f32),
            pltpu.VMEM((WAYS, 96, LANES), f32),
            pltpu.VMEM((WAYS, 32, LANES), f32),
            pltpu.VMEM(((SLOTS + 4) * SPAN, LANES), f32),
            pltpu.VMEM(((SLOTS + 4) * SPAN, LANES), f32),
            pltpu.VMEM(((SLOTS + 4) * 24, LANES), f32),
            pltpu.VMEM((4 * Z_ROWS, 256), f32),
            pltpu.VMEM((SPAN, SPAN, 4 * LANES), jnp.bfloat16),
        ],
        compiler_params=pltpu.CompilerParams(vmem_limit_bytes=40 * 1024 * 1024),
        name="field_and_forces",
    )(meta, box_scale, atoms.reshape(SOURCES * ROWS, LANES))


def exchange_kernel(pos_ref, q_ref, anchor_ref, atoms_ref, blocks_ref, atoms_out, meta_out, send_sems, recv_sems):
    me = {a: lax.axis_index(a) for a in ("gx", "gy", "gz")}
    def near(axis, step):
        n = lax.axis_size(axis)
        return {axis: lax.rem(me[axis] + step + n, n)}
    barrier = pltpu.get_barrier_semaphore()
    for axis in ("gy", "gz", "gx"):
        for step in (1, -1):
            pl.semaphore_signal(barrier, inc=1, device_id=near(axis, step), device_id_type=MESH)
    far = {1: lax.rem(me["gy"], 4) == 3, -1: lax.rem(me["gy"], 4) == 0}
    wrap = {1: me["gz"] == lax.axis_size("gz") - 1, -1: me["gz"] == 0}
    corners = [(sy, sz) for sy in (1, -1) for sz in (1, -1)]
    def corner_id(sy, sz):
        return {**near("gy", sy), **near("gz", sz)}
    for sy, sz in corners:
        @pl.when(far[sy] & wrap[sz])
        def _():
            pl.semaphore_signal(barrier, inc=1, device_id=corner_id(sy, sz), device_id_type=MESH)
    for a in range(3):
        for b in range(8):
            atoms_out[0, pl.ds(a * 8 + b, 1), :] = pos_ref[pl.ds(a, 1), pl.ds(b * 128, 128)]
    row = lax.broadcasted_iota(jnp.int32, (8, 128), 0)
    lane = lax.broadcasted_iota(jnp.int32, (8, 128), 1)
    filled = jnp.zeros((8, 128), jnp.int32)
    for b in range(8):
        filled = jnp.where(row == b, jnp.where(b < blocks_ref[0], atoms_ref[b], 0), filled)
    atoms_out[0, pl.ds(24, 8), :] = jnp.where(lane < filled, q_ref[...], 0.0)
    meta = jnp.zeros((8, 128), jnp.int32)
    for a in range(3):
        for b in range(8):
            meta = jnp.where(lane == a * 8 + b, anchor_ref[a, b], meta)
    for b in range(8):
        meta = jnp.where(lane == 24 + b, jnp.where(b < blocks_ref[0], 1, 0), meta)
    atoms_out[0, pl.ds(32, 8), :] = meta.astype(jnp.float32)
    at_corner = (far[1] | far[-1]) & (wrap[1] | wrap[-1])
    pl.semaphore_wait(barrier, 6 + at_corner.astype(jnp.int32))

    def slot(cx, cz, cy):
        return (cx * 3 + cz) * 3 + cy
    code = {1: 1, -1: 2}
    def piece(src, dst, target, send_index=None):
        return pltpu.make_async_remote_copy(
            src_ref=atoms_out.at[src], dst_ref=atoms_out.at[dst],
            send_sem=send_sems.at[dst if send_index is None else send_index], recv_sem=recv_sems.at[dst],
            device_id=target, device_id_type=MESH)
    def y_piece(step):
        return piece(0, slot(0, 0, code[step]), near("gy", step))
    def z_piece(cy, step):
        return piece(slot(0, 0, cy), slot(0, code[step], cy), near("gz", step))
    def x_piece(cz, cy, step):
        return piece(slot(0, cz, cy), slot(code[step], cz, cy), near("gx", step))
    def corner_piece(k, sy, sz):
        return piece(0, slot(0, code[sz], code[sy]), corner_id(sy, sz), 27 + k)
    def relays(cy, step):
        return jnp.logical_not((far[-1] if cy == 1 else far[1]) & wrap[step])
    for step in (1, -1):
        y_piece(step).start()
    for k, (sy, sz) in enumerate(corners):
        @pl.when(far[sy] & wrap[sz])
        def _():
            corner_piece(k, sy, sz).start()
    for step in (1, -1):
        z_piece(0, step).start()
    for step in (1, -1):
        x_piece(0, 0, step).start()
    def send_y_on(cy):
        y_piece(1 if cy == 1 else -1).wait_recv()
        for step in (1, -1):
            @pl.when(relays(cy, step))
            def _():
                z_piece(cy, step).start()
        for step in (1, -1):
            x_piece(0, cy, step).start()
    def send_z_on(cz, cy):
        z_piece(cy, 1 if cz == 1 else -1).wait_recv()
        for step in (1, -1):
            x_piece(cz, cy, step).start()
    low = lax.rem(me["gy"], 4) == 0
    @pl.when(low)
    def _():
        send_y_on(2)
        send_z_on(1, 0)
        send_z_on(2, 0)
        send_z_on(1, 2)
        send_z_on(2, 2)
        send_y_on(1)
        send_z_on(1, 1)
        send_z_on(2, 1)
    @pl.when(jnp.logical_not(low))
    def _():
        send_y_on(1)
        send_z_on(1, 0)
        send_z_on(2, 0)
        send_z_on(1, 1)
        send_z_on(2, 1)
        send_y_on(2)
        send_z_on(1, 2)
        send_z_on(2, 2)
    for step in (1, -1):
        for cz in range(3):
            for cy in range(3):
                x_piece(cz, cy, step).wait_recv()
    for step in (1, -1):
        y_piece(step).wait_send()
        for cz in range(3):
            for cy in range(3):
                x_piece(cz, cy, step).wait_send()
        z_piece(0, step).wait_send()
        for cy in (1, 2):
            @pl.when(relays(cy, step))
            def _():
                z_piece(cy, step).wait_send()
    for k, (sy, sz) in enumerate(corners):
        @pl.when(far[sy] & wrap[sz])
        def _():
            corner_piece(k, sy, sz).wait_send()
    for n in range(27):
        meta_out[pl.ds(n, 1), :] = atoms_out[n, pl.ds(32, 1), :].astype(jnp.int32)

def exchange(positions, charges, block_anchor, block_atoms, brick_blocks):
    smem = pl.BlockSpec(memory_space=pltpu.SMEM)
    vmem = pl.BlockSpec(memory_space=pltpu.VMEM)
    return pl.pallas_call(
        exchange_kernel,
        out_shape=(jax.ShapeDtypeStruct((27, ROWS, 128), jnp.float32), jax.ShapeDtypeStruct((32, 128), jnp.int32)),
        in_specs=[vmem, vmem, smem, smem, smem],
        out_specs=(vmem, vmem),
        scratch_shapes=[pltpu.SemaphoreType.DMA((32,)), pltpu.SemaphoreType.DMA((27,))],
        compiler_params=pltpu.CompilerParams(collective_id=0, has_side_effects=True),
        name="exchange_atoms",
    )(positions, charges.reshape(8, 128), block_anchor, block_atoms, brick_blocks)


def per_device(positions, charges, block_anchor, block_atoms, brick_blocks, box_scale):
    atoms, meta = exchange(positions, charges, block_anchor, block_atoms, brick_blocks)
    potential, forces = make_field(atoms, meta, box_scale)
    return (potential, forces)


def solution(mesh):
    split_all = ("gx", "gy", "gz")
    return jax.shard_map(
        per_device,
        mesh=mesh,
        in_specs=(P(None, split_all), P(split_all), P(None, split_all), P(split_all), P(split_all), P()),
        out_specs=(P("gx", "gy", "gz"), P(None, split_all)),
        check_vma=False,
    )
```

time: 373 us -> 57.6 us (0.15)
  the two profiles are of different devices: /device:TPU:27 before, /device:TPU:13 now
where the time goes in v1:
time: 57.6 us; the launch traced here: 57.2 us
  Pallas kernels  53.5 us (93%)
  local copies, waits for them, and re-layouts  2.42 us (4%)
  between operations  1.3 us (2%)
    pallas_call x1, Pallas kernels, exchange(): pl.pallas_call(exchange_kernel, out_shape=(jax.ShapeDtypeStruct((27, ROWS...  36.9 us
    pallas_call x1, Pallas kernels, make_field(): pl.pallas_call(field_kernel, out_shape=(jax.ShapeDtypeStruct((CX, CY, CZ)...  16.6 us
    unnamed x6, local copies, waits for them, and re-layouts  2.42 us

profile of v1, /device:TPU:13, one launch (start us, length us, event | category | flops | bytes accessed | tf_op | source)
XLA Modules:
  0.0 57.2 jit_solution(1578051983243601633)
XLA Ops:
  1.3 36.9 %exchange_atoms.1 = (f32[27,40,128]{2,1,0:T(8,128)}, s32[32,128]{1,0:T(8,128)}) custom-call(f32[3,1024]{1,0:T(4,128)} %pos_ref.1, f32[8,128]{1,0:T(8,128)} %bitcast.3, s32[3,8]{1,0:T(4,128)} %anchor_ref.1, s32[8]{0:T(128)} %atoms_ref.1, s32[1]{0:T(128)S(6)} %copy.8.blocks_ref), custom_call_target="tpu_custom_call" | custom-call | tf_op jit(solution)/shard_map/exchange_atoms/pallas_call | solution.py:367
  38.2 0.0 copy-start.2
  38.2 0.6 %copy-done.2 = f32[3]{0:T(128)S(1)} copy-done((f32[3]{0:T(128)S(1)}, f32[3]{0:T(128)}, u32[]{:S(2)}) %copy-start.2) | copy-done | bytes 36
  38.9 0.0 copy-start
  38.9 1.0 %copy-done = f32[27,40,128]{2,1,0:T(8,128)S(1)} copy-done((f32[27,40,128]{2,1,0:T(8,128)S(1)}, f32[27,40,128]{2,1,0:T(8,128)}, u32[]{:S(2)}) %copy-start) | copy-done | bytes 552984
  39.9 0.0 copy-start.1
  39.9 0.7 %copy-done.1 = s32[32,128]{1,0:T(8,128)S(1)} copy-done((s32[32,128]{1,0:T(8,128)S(1)}, s32[32,128]{1,0:T(8,128)}, u32[]{:S(2)}) %copy-start.1) | copy-done | bytes 16408
  40.6 16.6 %field_and_forces.1 = (f32[24,24,128]{2,1,0:T(8,128)}, f32[3,1024]{1,0:T(4,128)}) custom-call(s32[32,128]{1,0:T(8,128)S(1)} %copy-done.1, f32[3]{0:T(128)S(1)} %copy-done.2, f32[1080,128]{1,0:T(8,128)S(1)} %bitcast.2), custom_call_target="tpu_custom_call" | custom-call | tf_op jit(solution)/shard_map/field_and_forces/pallas_call | solution.py:222
Async XLA Ops:
  38.2 0.7 %copy-start.2 = (f32[3]{0:T(128)S(1)}, f32[3]{0:T(128)}, u32[]{:S(2)}) copy-start(f32[3]{0:T(128)} %scale_ref.1) | copy-start | bytes 40
  38.9 1.1 %copy-start = (f32[27,40,128]{2,1,0:T(8,128)S(1)}, f32[27,40,128]{2,1,0:T(8,128)}, u32[]{:S(2)}) copy-start(f32[27,40,128]{2,1,0:T(8,128)} %get-tuple-element.5) | copy-start | bytes 1658884
  39.9 0.7 %copy-start.1 = (s32[32,128]{1,0:T(8,128)S(1)}, s32[32,128]{1,0:T(8,128)}, u32[]{:S(2)}) copy-start(s32[32,128]{1,0:T(8,128)} %get-tuple-element.4.meta) | copy-start | bytes 49156

commit v2 on v1

--- a/solution.py
+++ b/solution.py
@@ -242,24 +242,55 @@
     )(meta, box_scale, atoms.reshape(SOURCES * ROWS, LANES))
 
 
-def exchange_kernel(pos_ref, q_ref, anchor_ref, atoms_ref, blocks_ref, atoms_out, meta_out, send_sems, recv_sems):
-    me = {a: lax.axis_index(a) for a in ("gx", "gy", "gz")}
-    def near(axis, step):
-        n = lax.axis_size(axis)
-        return {axis: lax.rem(me[axis] + step + n, n)}
+def exchange_kernel(pos_ref, q_ref, anchor_ref, atoms_ref, blocks_ref, atoms_out, meta_out, send_sems, recv_sems, ready_sems):
+    gx, gy, gz = (lax.axis_index(a) for a in ("gx", "gy", "gz"))
+    nx, ny, nz = (lax.axis_size(a) for a in ("gx", "gy", "gz"))
+    half = ny // 2
+
+    def device(dx, dy, dz):
+        return (lax.rem(gx + dx + nx, nx), lax.rem(gy + dy + ny, ny), lax.rem(gz + dz + nz, nz))
+
+    late = gy >= half
+    far = {1: lax.rem(gy, half) == half - 1, -1: lax.rem(gy, half) == 0}
+    wrap = {1: gz == nz - 1, -1: gz == 0}
+    far_any = far[1] | far[-1]
+    corner = far_any & (wrap[1] | wrap[-1])
+    far_step = jnp.where(far[1], 1, -1)
+    wrap_step = jnp.where(wrap[1], 1, -1)
+    steps = (1, -1)
+    code = {1: 1, -1: 2}
+    across = (0, 1, -1)
+    ready_z, ready_y, ready_c = (ready_sems.at[i] for i in range(3))
+
+    def when(condition, action):
+        pl.when(condition)(action)
+
+    def both(condition, other):
+        return condition & jnp.logical_not(other)
+
+    def signal(semaphore, *offsets):
+        pl.semaphore_signal(semaphore, inc=1, device_id=device(*offsets), device_id_type=MESH)
+
     barrier = pltpu.get_barrier_semaphore()
-    for axis in ("gy", "gz", "gx"):
-        for step in (1, -1):
-            pl.semaphore_signal(barrier, inc=1, device_id=near(axis, step), device_id_type=MESH)
-    far = {1: lax.rem(me["gy"], 4) == 3, -1: lax.rem(me["gy"], 4) == 0}
-    wrap = {1: me["gz"] == lax.axis_size("gz") - 1, -1: me["gz"] == 0}
-    corners = [(sy, sz) for sy in (1, -1) for sz in (1, -1)]
-    def corner_id(sy, sz):
-        return {**near("gy", sy), **near("gz", sz)}
-    for sy, sz in corners:
-        @pl.when(far[sy] & wrap[sz])
-        def _():
-            pl.semaphore_signal(barrier, inc=1, device_id=corner_id(sy, sz), device_id_type=MESH)
+
+    def greet_far():
+        signal(barrier, 0, far_step, 0)
+
+    def greet_corner():
+        for dx in across:
+            signal(barrier, dx, far_step, wrap_step)
+
+    def greet_wrap(step):
+        for dx in across:
+            signal(barrier, dx, 0, step)
+
+    when(both(far_any, late), greet_far)
+    when(both(corner, late), greet_corner)
+    for step in steps:
+        signal(barrier, step, 0, 0)
+        when(jnp.logical_not(far[step]), lambda: signal(barrier, 0, step, 0))
+    greet_wrap(-1)
+    when(jnp.logical_not(wrap[1]), lambda: greet_wrap(1))
     for a in range(3):
         for b in range(8):
             atoms_out[0, pl.ds(a * 8 + b, 1), :] = pos_ref[pl.ds(a, 1), pl.ds(b * 128, 128)]
@@ -276,88 +307,112 @@
     for b in range(8):
         meta = jnp.where(lane == 24 + b, jnp.where(b < blocks_ref[0], 1, 0), meta)
     atoms_out[0, pl.ds(32, 8), :] = meta.astype(jnp.float32)
-    at_corner = (far[1] | far[-1]) & (wrap[1] | wrap[-1])
-    pl.semaphore_wait(barrier, 6 + at_corner.astype(jnp.int32))
+    peers = 7 + jnp.where(wrap[-1], 0, 3) - jnp.where(both(far_any, late), 1, 0) + jnp.where(corner & late, 3, 0)
+    pl.semaphore_wait(barrier, peers)
+
+    def answer_wrap():
+        for dx in across:
+            signal(ready_z, dx, 0, 1)
+
+    def answer_corner():
+        for dx in across:
+            signal(ready_c, dx, far_step, wrap_step)
+
+    when(far_any & late, lambda: signal(ready_y, 0, far_step, 0))
+    when(wrap[1], answer_wrap)
+    when(corner & late, answer_corner)
 
     def slot(cx, cz, cy):
         return (cx * 3 + cz) * 3 + cy
-    code = {1: 1, -1: 2}
-    def piece(src, dst, target, send_index=None):
+
+    def piece(src, dst, target, index):
         return pltpu.make_async_remote_copy(
             src_ref=atoms_out.at[src], dst_ref=atoms_out.at[dst],
-            send_sem=send_sems.at[dst if send_index is None else send_index], recv_sem=recv_sems.at[dst],
+            send_sem=send_sems.at[index], recv_sem=recv_sems.at[dst],
             device_id=target, device_id_type=MESH)
-    def y_piece(step):
-        return piece(0, slot(0, 0, code[step]), near("gy", step))
-    def z_piece(cy, step):
-        return piece(slot(0, 0, cy), slot(0, code[step], cy), near("gz", step))
-    def x_piece(cz, cy, step):
-        return piece(slot(0, cz, cy), slot(code[step], cz, cy), near("gx", step))
-    def corner_piece(k, sy, sz):
-        return piece(0, slot(0, code[sz], code[sy]), corner_id(sy, sz), 27 + k)
-    def relays(cy, step):
-        return jnp.logical_not((far[-1] if cy == 1 else far[1]) & wrap[step])
-    for step in (1, -1):
-        y_piece(step).start()
-    for k, (sy, sz) in enumerate(corners):
-        @pl.when(far[sy] & wrap[sz])
-        def _():
-            corner_piece(k, sy, sz).start()
-    for step in (1, -1):
-        z_piece(0, step).start()
-    for step in (1, -1):
-        x_piece(0, 0, step).start()
-    def send_y_on(cy):
-        y_piece(1 if cy == 1 else -1).wait_recv()
-        for step in (1, -1):
-            @pl.when(relays(cy, step))
-            def _():
-                z_piece(cy, step).start()
-        for step in (1, -1):
-            x_piece(0, cy, step).start()
-    def send_z_on(cz, cy):
-        z_piece(cy, 1 if cz == 1 else -1).wait_recv()
-        for step in (1, -1):
-            x_piece(cz, cy, step).start()
-    low = lax.rem(me["gy"], 4) == 0
-    @pl.when(low)
-    def _():
-        send_y_on(2)
-        send_z_on(1, 0)
-        send_z_on(2, 0)
-        send_z_on(1, 2)
-        send_z_on(2, 2)
-        send_y_on(1)
-        send_z_on(1, 1)
-        send_z_on(2, 1)
-    @pl.when(jnp.logical_not(low))
-    def _():
-        send_y_on(1)
-        send_z_on(1, 0)
-        send_z_on(2, 0)
-        send_z_on(1, 1)
-        send_z_on(2, 1)
-        send_y_on(2)
-        send_z_on(1, 2)
-        send_z_on(2, 2)
-    for step in (1, -1):
-        for cz in range(3):
-            for cy in range(3):
-                x_piece(cz, cy, step).wait_recv()
-    for step in (1, -1):
-        y_piece(step).wait_send()
-        for cz in range(3):
-            for cy in range(3):
-                x_piece(cz, cy, step).wait_send()
-        z_piece(0, step).wait_send()
+
+    def along_y(step):
+        dst = slot(0, 0, code[step])
+        return [piece(0, dst, device(0, step, 0), dst)]
+
+    def along_x(cy):
+        return [piece(cy, slot(code[dx], 0, cy), device(dx, 0, 0), slot(code[dx], 0, cy)) for dx in steps]
+
+    def fan(cy, step):
+        places = [(dx, slot(code[dx] if dx else 0, code[step], cy)) for dx in across]
+        return [piece(cy, dst, device(dx, 0, step), dst) for dx, dst in places]
+
+    def corners():
+        out = []
+        for i, dx in enumerate(across):
+            dst = slot(code[dx] if dx else 0, jnp.where(wrap[1], 1, 2), jnp.where(far[1], 1, 2))
+            out.append(piece(0, dst, device(dx, far_step, wrap_step), 27 + i))
+        return out
+
+    def start(copies):
+        for copy in copies:
+            copy.start()
+
+    def finish(copies):
+        for copy in copies:
+            copy.wait_send()
+
+    from_far = {1: far[-1], 2: far[1]}
+
+    def send_early(cy):
+        start(along_x(cy))
+        start(fan(cy, 1))
+        when(jnp.logical_not(wrap[-1]), lambda: start(fan(cy, -1)))
+
+    def pass_near(cy):
+        along_y(1 if cy == 1 else -1)[0].wait_recv()
+        send_early(cy)
+
+    def pass_far(cy):
+        along_y(1 if cy == 1 else -1)[0].wait_recv()
+        start(along_x(cy))
+        for step in steps:
+            when(jnp.logical_not(wrap[step]), lambda: start(fan(cy, step)))
+
+    def open_wrap():
+        pl.semaphore_wait(ready_z, 3)
+        start(fan(0, -1))
         for cy in (1, 2):
-            @pl.when(relays(cy, step))
-            def _():
-                z_piece(cy, step).wait_send()
-    for k, (sy, sz) in enumerate(corners):
-        @pl.when(far[sy] & wrap[sz])
-        def _():
-            corner_piece(k, sy, sz).wait_send()
+            when(jnp.logical_not(from_far[cy]), lambda: start(fan(cy, -1)))
+
+    def open_corner():
+        pl.semaphore_wait(ready_c, 3)
+        start(corners())
+
+    def open_far():
+        pl.semaphore_wait(ready_y, 1)
+        for step in steps:
+            when(far[step], lambda: start(along_y(step)))
+
+    for step in steps:
+        when(jnp.logical_not(both(far[step], late)), lambda: start(along_y(step)))
+    when(corner & late, lambda: start(corners()))
+    send_early(0)
+    for cy in (1, 2):
+        when(jnp.logical_not(from_far[cy]), lambda: pass_near(cy))
+    when(wrap[-1], open_wrap)
+    when(both(corner, late), open_corner)
+    when(both(far_any, late), open_far)
+    for cy in (1, 2):
+        when(from_far[cy], lambda: pass_far(cy))
+    for cy in range(3):
+        for copy in along_x(cy) + fan(cy, 1) + fan(cy, -1):
+            copy.wait_recv()
+    for step in steps:
+        finish(along_y(step))
+    for cy in range(3):
+        finish(along_x(cy))
+        for step in steps:
+            if cy == 0:
+                finish(fan(cy, step))
+            else:
+                when(jnp.logical_not(from_far[cy] & wrap[step]), lambda: finish(fan(cy, step)))
+    when(corner, lambda: finish(corners()))
     for n in range(27):
         meta_out[pl.ds(n, 1), :] = atoms_out[n, pl.ds(32, 1), :].astype(jnp.int32)
 
@@ -369,7 +424,8 @@
         out_shape=(jax.ShapeDtypeStruct((27, ROWS, 128), jnp.float32), jax.ShapeDtypeStruct((32, 128), jnp.int32)),
         in_specs=[vmem, vmem, smem, smem, smem],
         out_specs=(vmem, vmem),
-        scratch_shapes=[pltpu.SemaphoreType.DMA((32,)), pltpu.SemaphoreType.DMA((27,))],
+        scratch_shapes=[pltpu.SemaphoreType.DMA((32,)), pltpu.SemaphoreType.DMA((27,)),
+                        pltpu.SemaphoreType.REGULAR((3,))],
         compiler_params=pltpu.CompilerParams(collective_id=0, has_side_effects=True),
         name="exchange_atoms",
     )(positions, charges.reshape(8, 128), block_anchor, block_atoms, brick_blocks)

time: 57.6 us -> 50.6 us (0.88)
  the two profiles are of different devices: /device:TPU:13 before, /device:TPU:417 now
where the time goes in v2:
time: 50.6 us; the launch traced here: 50.3 us
  Pallas kernels  46.6 us (92%)
  local copies, waits for them, and re-layouts  2.42 us (5%)
  between operations  1.3 us (3%)
    pallas_call x1, Pallas kernels, exchange(): pl.pallas_call(exchange_kernel, out_shape=(jax.ShapeDtypeStruct((27, ROWS...  29.7 us
    pallas_call x1, Pallas kernels, make_field(): pl.pallas_call(field_kernel, out_shape=(jax.ShapeDtypeStruct((CX, CY, CZ)...  16.9 us
    unnamed x6, local copies, waits for them, and re-layouts  2.42 us

profile of v2, /device:TPU:417, one launch (start us, length us, event | category | flops | bytes accessed | tf_op | source)
XLA Modules:
  0.0 50.3 jit_solution(206859740716818122)
XLA Ops:
  1.3 29.7 %exchange_atoms.1 = (f32[27,40,128]{2,1,0:T(8,128)}, s32[32,128]{1,0:T(8,128)}) custom-call(f32[3,1024]{1,0:T(4,128)} %pos_ref.1, f32[8,128]{1,0:T(8,128)} %bitcast.3, s32[3,8]{1,0:T(4,128)} %anchor_ref.1, s32[8]{0:T(128)} %atoms_ref.1, s32[1]{0:T(128)S(6)} %copy.8.blocks_ref), custom_call_target="tpu_custom_call" | custom-call | tf_op jit(solution)/shard_map/exchange_atoms/pallas_call | solution.py:422
  31.0 0.0 copy-start.2
  31.0 0.6 %copy-done.2 = f32[3]{0:T(128)S(1)} copy-done((f32[3]{0:T(128)S(1)}, f32[3]{0:T(128)}, u32[]{:S(2)}) %copy-start.2) | copy-done | bytes 36
  31.6 0.0 copy-start
  31.6 1.0 %copy-done = f32[27,40,128]{2,1,0:T(8,128)S(1)} copy-done((f32[27,40,128]{2,1,0:T(8,128)S(1)}, f32[27,40,128]{2,1,0:T(8,128)}, u32[]{:S(2)}) %copy-start) | copy-done | bytes 552984
  32.7 0.0 copy-start.1
  32.7 0.7 %copy-done.1 = s32[32,128]{1,0:T(8,128)S(1)} copy-done((s32[32,128]{1,0:T(8,128)S(1)}, s32[32,128]{1,0:T(8,128)}, u32[]{:S(2)}) %copy-start.1) | copy-done | bytes 16408
  33.4 16.9 %field_and_forces.1 = (f32[24,24,128]{2,1,0:T(8,128)}, f32[3,1024]{1,0:T(4,128)}) custom-call(s32[32,128]{1,0:T(8,128)S(1)} %copy-done.1, f32[3]{0:T(128)S(1)} %copy-done.2, f32[1080,128]{1,0:T(8,128)S(1)} %bitcast.2), custom_call_target="tpu_custom_call" | custom-call | tf_op jit(solution)/shard_map/field_and_forces/pallas_call | solution.py:222
Async XLA Ops:
  31.0 0.7 %copy-start.2 = (f32[3]{0:T(128)S(1)}, f32[3]{0:T(128)}, u32[]{:S(2)}) copy-start(f32[3]{0:T(128)} %scale_ref.1) | copy-start | bytes 40
  31.6 1.1 %copy-start = (f32[27,40,128]{2,1,0:T(8,128)S(1)}, f32[27,40,128]{2,1,0:T(8,128)}, u32[]{:S(2)}) copy-start(f32[27,40,128]{2,1,0:T(8,128)} %get-tuple-element.5) | copy-start | bytes 1658884
  32.7 0.7 %copy-start.1 = (s32[32,128]{1,0:T(8,128)S(1)}, s32[32,128]{1,0:T(8,128)}, u32[]{:S(2)}) copy-start(s32[32,128]{1,0:T(8,128)} %get-tuple-element.4.meta) | copy-start | bytes 49156

commit v3 on v2

--- a/solution.py
+++ b/solution.py
@@ -16,14 +16,16 @@
 SPREAD = 1.0
 SMOOTH = 1.5
 COUPLING = 200.0
-ROWS = 40
+ROWS = 33
+ONE_SIDED = 3
 BLOCKS = 8
 LANES = 128
 SOURCES = 27
 SLOTS = SOURCES * BLOCKS
 SPAN = 32
 Z_ROWS = 176
-WAYS = 4
+WAYS = 16
+EMPTY = SLOTS + WAYS
 PAD = 40
 
 
@@ -44,45 +46,37 @@
     return high, (value - high.astype(jnp.float32)).astype(jnp.bfloat16)
 
 
-def field_kernel(meta, scale_ref, atoms, potential, forces, order, tasks, starts, pad_x, pad_y, pad_z, wx_all, wy_all, wz_all, density, field):
+def field_kernel(meta_in, atoms_in, potential, forces, meta, atoms, load_sems, order, tasks, starts, pad_x, pad_y, pad_z, wx_all, wy_all, wz_all, density, field):
     f32 = jnp.float32
-    scales = [jnp.full((1, LANES), scale_ref[a], f32) for a in range(3)]
+    load_meta = pltpu.make_async_copy(meta_in, meta, load_sems.at[0])
+    load_meta.start()
+    load_atoms = pltpu.make_async_copy(atoms_in, atoms, load_sems.at[1])
+    load_atoms.start()
+    density[...] = jnp.zeros_like(density)
+    for ref in (pad_x, pad_y, pad_z):
+        ref[...] = jnp.zeros_like(ref)
+    wx_all[pl.ds(EMPTY * SPAN, SPAN), :] = jnp.zeros((SPAN, LANES), f32)
+    wy_all[pl.ds(EMPTY * SPAN, SPAN), :] = jnp.zeros((SPAN, LANES), f32)
+    wz_all[pl.ds(EMPTY * 24, 24), :] = jnp.zeros((24, LANES), f32)
+    starts[EMPTY] = 0
+    load_meta.wait()
+
+    def choose(n, count):
+        for b in range(BLOCKS):
+            order[count] = n * BLOCKS + b
+            count = count + meta[n, 4 * BLOCKS + b]
+        return count
+
+    blocks = lax.fori_loop(0, SOURCES, choose, jnp.int32(0))
+    for extra in range(WAYS - 1):
+        order[blocks + extra] = 0
+    load_atoms.wait()
+    scales = [atoms[SOURCES, pl.ds(a, 1), :] for a in range(3)]
     widths = [SPREAD * s for s in scales]
     taps = []
     for a in range(3):
         tau = SMOOTH * scales[a]
         taps.append([jnp.exp(-float(e * e) / (2.0 * tau * tau)) * norm(tau) for e in range(RADIUS + 1)])
-    density[...] = jnp.zeros_like(density)
-    for ref in (pad_x, pad_y, pad_z):
-        ref[...] = jnp.zeros_like(ref)
-    wx_all[pl.ds(SLOTS * SPAN, SPAN), :] = jnp.zeros((SPAN, LANES), f32)
-    wy_all[pl.ds(SLOTS * SPAN, SPAN), :] = jnp.zeros((SPAN, LANES), f32)
-    wz_all[pl.ds(SLOTS * 24, 24), :] = jnp.zeros((24, LANES), f32)
-    starts[SLOTS] = 0
-
-    def choose(n, count):
-        cx = n // 9
-        cz = n // 3 % 3
-        cy = n % 3
-        low_x = jnp.where(cx == 1, 5, 0)
-        high_x = jnp.where(cx == 2, 11, 999)
-        low_y = jnp.where(cy == 1, 5, 0)
-        high_y = jnp.where(cy == 2, 11, 999)
-        low_z = jnp.where(cz == 1, CZ - 19, 0)
-        high_z = jnp.where(cz == 2, 11, 999)
-        for b in range(BLOCKS):
-            x = meta[n, b]
-            y = meta[n, BLOCKS + b]
-            z = meta[n, 2 * BLOCKS + b]
-            live = meta[n, 3 * BLOCKS + b]
-            near = (x >= low_x) & (x <= high_x) & (y >= low_y) & (y <= high_y) & (z >= low_z) & (z <= high_z) & (live > 0)
-            order[count] = n * BLOCKS + b
-            count = count + near.astype(jnp.int32)
-        return count
-
-    blocks = lax.fori_loop(0, SOURCES, choose, jnp.int32(0))
-    for extra in range(WAYS - 1):
-        order[blocks + extra] = 0
 
     iota16 = lax.broadcasted_iota(jnp.int32, (PATCH, LANES), 0)
 
@@ -93,16 +87,14 @@
             n = code // BLOCKS
             b = code % BLOCKS
             cx = n // 9
-            cz = n // 3 % 3
             cy = n % 3
-            off_x = meta[n, b] + jnp.where(cx == 0, 0, jnp.where(cx == 1, -CX, CX))
-            off_y = meta[n, BLOCKS + b] + jnp.where(cy == 0, 0, jnp.where(cy == 1, -CY, CY))
-            off_z = meta[n, 2 * BLOCKS + b] + jnp.where(cz == 0, 0, jnp.where(cz == 1, -CZ, CZ))
-            row = n * ROWS + b
-            x = atoms[pl.ds(row, 1), :] * scales[0]
-            y = atoms[pl.ds(row + BLOCKS, 1), :] * scales[1]
-            z = atoms[pl.ds(row + 2 * BLOCKS, 1), :] * scales[2]
-            q = atoms[pl.ds(row + 3 * BLOCKS, 1), :]
+            off_x = meta[n, b]
+            off_y = meta[n, BLOCKS + b]
+            off_z = meta[n, 2 * BLOCKS + b]
+            x = atoms[n, pl.ds(b, 1), :] * scales[0]
+            y = atoms[n, pl.ds(b + BLOCKS, 1), :] * scales[1]
+            z = atoms[n, pl.ds(b + 2 * BLOCKS, 1), :] * scales[2]
+            q = atoms[n, pl.ds(b + 3 * BLOCKS, 1), :]
             pad_x[way, pl.ds(PAD, PATCH), :] = q * window(x, iota16, widths[0])[0]
             pad_y[way, pl.ds(PAD, PATCH), :] = window(y, iota16, widths[1])[0]
             pad_z[way, pl.ds(8, PATCH), :] = window(z, iota16, widths[2])[0]
@@ -113,7 +105,7 @@
                     total = total + taps[a][e] * (pad[way, pl.ds(start - e, SPAN), :] + pad[way, pl.ds(start + e, SPAN), :])
                 out[pl.ds(pl.multiple_of(k * SPAN, SPAN), SPAN), :] = total
             first = off_z + 20
-            shift = first % 8
+            shift = first & 7
             wz_all[pl.ds(pl.multiple_of(k * 24, 8), 24), :] = pad_z[way, pl.ds(8 - shift, 24), :]
             starts[k] = first - shift
             used = k < blocks
@@ -126,7 +118,7 @@
 
     jobs = lax.fori_loop(0, (blocks + WAYS - 1) // WAYS, weigh, jnp.int32(0))
     for extra in range(WAYS - 1):
-        tasks[jobs + extra] = SLOTS * 4
+        tasks[jobs + extra] = EMPTY * 4
 
     def spread(group, carry):
         for way in range(WAYS):
@@ -152,9 +144,8 @@
 
     length = CZ + 2 * (RIM + RADIUS)
     gap = lax.broadcasted_iota(jnp.int32, (length, length), 0) - lax.broadcasted_iota(jnp.int32, (length, length), 1)
-    tau = SMOOTH * scale_ref[2]
     gap_f = gap.astype(f32)
-    tau_v = jnp.full((length, length), tau, f32)
+    tau_v = jnp.broadcast_to(SMOOTH * scales[2][:, :1], (length, length))
     band = jnp.exp(-gap_f * gap_f / (2.0 * tau_v * tau_v)) * (COUPLING / (math.sqrt(2.0 * math.pi) * tau_v))
     band_high, band_low = split(jnp.where(jnp.abs(gap) <= RADIUS, band, 0.0))
     for half in range(2):
@@ -182,10 +173,10 @@
     edge_z = jnp.where(iota8 < 4, iota8 - 4, iota8 + (CZ - 4))
 
     def force(b):
-        x = atoms[pl.ds(b, 1), :] * scales[0]
-        y = atoms[pl.ds(b + BLOCKS, 1), :] * scales[1]
-        z = atoms[pl.ds(b + 2 * BLOCKS, 1), :] * scales[2]
-        q = atoms[pl.ds(b + 3 * BLOCKS, 1), :]
+        x = atoms[0, pl.ds(b, 1), :] * scales[0]
+        y = atoms[0, pl.ds(b + BLOCKS, 1), :] * scales[1]
+        z = atoms[0, pl.ds(b + 2 * BLOCKS, 1), :] * scales[2]
+        q = atoms[0, pl.ds(b + 3 * BLOCKS, 1), :]
         at_x = meta[0, b]
         at_y = meta[0, BLOCKS + b]
         at_z = meta[0, 2 * BLOCKS + b]
@@ -215,46 +206,60 @@
         force(b)
 
 
-def make_field(atoms, meta, box_scale):
-    smem = pl.BlockSpec(memory_space=pltpu.SMEM)
+def make_field(atoms, meta):
+    anywhere = pl.BlockSpec(memory_space=pl.ANY)
     vmem = pl.BlockSpec(memory_space=pltpu.VMEM)
-    f32 = jnp.float32
+    f32, i32 = jnp.float32, jnp.int32
     return pl.pallas_call(
         field_kernel,
         out_shape=(jax.ShapeDtypeStruct((CX, CY, CZ), f32), jax.ShapeDtypeStruct((3, BLOCKS * LANES), f32)),
-        in_specs=[smem, smem, vmem],
+        in_specs=[anywhere, anywhere],
         out_specs=(vmem, vmem),
         scratch_shapes=[
-            pltpu.SMEM((SLOTS + 8,), jnp.int32),
-            pltpu.SMEM((SLOTS * 4 + 8,), jnp.int32),
-            pltpu.SMEM((SLOTS + 8,), jnp.int32),
+            pltpu.SMEM((32, LANES), i32),
+            pltpu.VMEM((SOURCES + 1, ROWS, LANES), f32),
+            pltpu.SemaphoreType.DMA((2,)),
+            pltpu.SMEM((EMPTY + 1,), i32),
+            pltpu.SMEM((SLOTS * 4 + WAYS,), i32),
+            pltpu.SMEM((EMPTY + 1,), i32),
             pltpu.VMEM((WAYS, 96, LANES), f32),
             pltpu.VMEM((WAYS, 96, LANES), f32),
             pltpu.VMEM((WAYS, 32, LANES), f32),
-            pltpu.VMEM(((SLOTS + 4) * SPAN, LANES), f32),
-            pltpu.VMEM(((SLOTS + 4) * SPAN, LANES), f32),
-            pltpu.VMEM(((SLOTS + 4) * 24, LANES), f32),
+            pltpu.VMEM(((EMPTY + 1) * SPAN, LANES), f32),
+            pltpu.VMEM(((EMPTY + 1) * SPAN, LANES), f32),
+            pltpu.VMEM(((EMPTY + 1) * 24, LANES), f32),
             pltpu.VMEM((4 * Z_ROWS, 256), f32),
             pltpu.VMEM((SPAN, SPAN, 4 * LANES), jnp.bfloat16),
         ],
         compiler_params=pltpu.CompilerParams(vmem_limit_bytes=40 * 1024 * 1024),
         name="field_and_forces",
-    )(meta, box_scale, atoms.reshape(SOURCES * ROWS, LANES))
-
-
-def exchange_kernel(pos_ref, q_ref, anchor_ref, atoms_ref, blocks_ref, atoms_out, meta_out, send_sems, recv_sems, ready_sems):
+    )(meta, atoms)
+
+
+def exchange_kernel(pos_in, q_in, anchor_in, atoms_in, blocks_in, scale_in, atoms_out, meta_out, pos_ref, q_ref, anchor_ref, atoms_ref, blocks_ref, scale_ref, rows_ref, load_sems, send_sems, recv_sems, ready_sems):
     gx, gy, gz = (lax.axis_index(a) for a in ("gx", "gy", "gz"))
     nx, ny, nz = (lax.axis_size(a) for a in ("gx", "gy", "gz"))
     half = ny // 2
 
     def device(dx, dy, dz):
         return (lax.rem(gx + dx + nx, nx), lax.rem(gy + dy + ny, ny), lax.rem(gz + dz + nz, nz))
+
+    def both(condition, other):
+        return condition & jnp.logical_not(other)
 
     late = gy >= half
     far = {1: lax.rem(gy, half) == half - 1, -1: lax.rem(gy, half) == 0}
     wrap = {1: gz == nz - 1, -1: gz == 0}
     far_any = far[1] | far[-1]
+    sided_y = gz < ONE_SIDED
+    sided_z = jnp.logical_not(late & jnp.logical_not(far_any))
+    hold = wrap[-1] & sided_z
+    ends = wrap[1] | wrap[-1]
+    direct = both(far_any, ends)
     corner = far_any & (wrap[1] | wrap[-1])
+    pushes = corner & late & wrap[-1]
+    pushed = both(corner & wrap[-1], late)
+    hands = both(corner, wrap[1] & jnp.logical_not(late))
     far_step = jnp.where(far[1], 1, -1)
     wrap_step = jnp.where(wrap[1], 1, -1)
     steps = (1, -1)
@@ -265,9 +270,6 @@
     def when(condition, action):
         pl.when(condition)(action)
 
-    def both(condition, other):
-        return condition & jnp.logical_not(other)
-
     def signal(semaphore, *offsets):
         pl.semaphore_signal(semaphore, inc=1, device_id=device(*offsets), device_id_type=MESH)
 
@@ -280,46 +282,49 @@
         for dx in across:
             signal(barrier, dx, far_step, wrap_step)
 
-    def greet_wrap(step):
-        for dx in across:
-            signal(barrier, dx, 0, step)
-
-    when(both(far_any, late), greet_far)
+    def greet_z(step):
+        signal(barrier, 0, 0, step)
+        for dx in steps:
+            when(jnp.logical_not(wrap[step]), lambda: signal(barrier, dx, 0, step))
+
+    when(both(direct, late & sided_y) | pushed, greet_far)
     when(both(corner, late), greet_corner)
     for step in steps:
         signal(barrier, step, 0, 0)
         when(jnp.logical_not(far[step]), lambda: signal(barrier, 0, step, 0))
-    greet_wrap(-1)
-    when(jnp.logical_not(wrap[1]), lambda: greet_wrap(1))
+    greet_z(-1)
+    when(jnp.logical_not(wrap[1] & sided_z), lambda: greet_z(1))
+    loads = []
+    for i, (src, dst) in enumerate(((pos_in, pos_ref), (q_in, q_ref), (anchor_in, anchor_ref), (atoms_in, atoms_ref), (blocks_in, blocks_ref), (scale_in, scale_ref))):
+        loads.append(pltpu.make_async_copy(src, dst, load_sems.at[i]))
+        loads[-1].start()
+    for load in loads:
+        load.wait()
     for a in range(3):
-        for b in range(8):
-            atoms_out[0, pl.ds(a * 8 + b, 1), :] = pos_ref[pl.ds(a, 1), pl.ds(b * 128, 128)]
-    row = lax.broadcasted_iota(jnp.int32, (8, 128), 0)
-    lane = lax.broadcasted_iota(jnp.int32, (8, 128), 1)
-    filled = jnp.zeros((8, 128), jnp.int32)
-    for b in range(8):
+        for b in range(BLOCKS):
+            atoms_out[0, pl.ds(a * BLOCKS + b, 1), :] = pos_ref[pl.ds(a, 1), pl.ds(b * LANES, LANES)]
+    row = lax.broadcasted_iota(jnp.int32, (BLOCKS, LANES), 0)
+    lane = lax.broadcasted_iota(jnp.int32, (BLOCKS, LANES), 1)
+    filled = jnp.zeros((BLOCKS, LANES), jnp.int32)
+    for b in range(BLOCKS):
         filled = jnp.where(row == b, jnp.where(b < blocks_ref[0], atoms_ref[b], 0), filled)
-    atoms_out[0, pl.ds(24, 8), :] = jnp.where(lane < filled, q_ref[...], 0.0)
-    meta = jnp.zeros((8, 128), jnp.int32)
+    atoms_out[0, pl.ds(3 * BLOCKS, BLOCKS), :] = jnp.where(lane < filled, q_ref[...], 0.0)
+    meta = jnp.zeros((BLOCKS, LANES), jnp.int32)
     for a in range(3):
-        for b in range(8):
-            meta = jnp.where(lane == a * 8 + b, anchor_ref[a, b], meta)
-    for b in range(8):
-        meta = jnp.where(lane == 24 + b, jnp.where(b < blocks_ref[0], 1, 0), meta)
-    atoms_out[0, pl.ds(32, 8), :] = meta.astype(jnp.float32)
-    peers = 7 + jnp.where(wrap[-1], 0, 3) - jnp.where(both(far_any, late), 1, 0) + jnp.where(corner & late, 3, 0)
+        for b in range(BLOCKS):
+            meta = jnp.where(lane == a * BLOCKS + b, anchor_ref[a, b], meta)
+    for b in range(BLOCKS):
+        meta = jnp.where(lane == 3 * BLOCKS + b, jnp.where(b < blocks_ref[0], 1, 0), meta)
+    atoms_out[0, pl.ds(32, 1), :] = meta[:1].astype(jnp.float32)
+    peers = 10 - jnp.where(hold, 3, jnp.where(ends, 2, 0)) - jnp.where(both(corner, pushes) | both(direct & sided_y, late), 1, 0) + jnp.where(corner & late, 3, 0)
     pl.semaphore_wait(barrier, peers)
-
-    def answer_wrap():
-        for dx in across:
-            signal(ready_z, dx, 0, 1)
 
     def answer_corner():
         for dx in across:
             signal(ready_c, dx, far_step, wrap_step)
 
-    when(far_any & late, lambda: signal(ready_y, 0, far_step, 0))
-    when(wrap[1], answer_wrap)
+    when(direct & late & sided_y, lambda: signal(ready_y, 0, far_step, 0))
+    when(wrap[1] & sided_z, lambda: signal(ready_z, 0, 0, 1))
     when(corner & late, answer_corner)
 
     def slot(cx, cz, cy):
@@ -361,8 +366,10 @@
 
     def send_early(cy):
         start(along_x(cy))
-        start(fan(cy, 1))
-        when(jnp.logical_not(wrap[-1]), lambda: start(fan(cy, -1)))
+        start(fan(cy, 1)[:1])
+        when(jnp.logical_not(hold), lambda: start(fan(cy, -1)[:1]))
+        for step in steps:
+            when(jnp.logical_not(wrap[step]), lambda: start(fan(cy, step)[1:]))
 
     def pass_near(cy):
         along_y(1 if cy == 1 else -1)[0].wait_recv()
@@ -375,14 +382,32 @@
             when(jnp.logical_not(wrap[step]), lambda: start(fan(cy, step)))
 
     def open_wrap():
-        pl.semaphore_wait(ready_z, 3)
-        start(fan(0, -1))
+        pl.semaphore_wait(ready_z, 1)
+        start(fan(0, -1)[:1])
         for cy in (1, 2):
-            when(jnp.logical_not(from_far[cy]), lambda: start(fan(cy, -1)))
+            when(jnp.logical_not(from_far[cy]), lambda: start(fan(cy, -1)[:1]))
+
+    def onward(cy, step):
+        src = slot(0, code[step], cy)
+        return [piece(src, slot(code[dx], code[step], cy), device(dx, 0, 0), 31 + cy * 2 + i) for i, dx in enumerate(steps)]
+
+    def pass_wrap(cy, step):
+        fan(cy, step)[0].wait_recv()
+        start(onward(cy, step))
 
     def open_corner():
         pl.semaphore_wait(ready_c, 3)
         start(corners())
+
+    def handed():
+        corner_slot = slot(0, jnp.where(wrap[1], 2, 1), jnp.where(far[1], 2, 1))
+        own_slot = slot(0, 0, jnp.where(far[1], 2, 1))
+        return piece(corner_slot, own_slot, device(0, 0, wrap_step), 30)
+
+    def forward_corner():
+        corner_slot = slot(0, jnp.where(wrap[1], 2, 1), jnp.where(far[1], 2, 1))
+        piece(corner_slot, corner_slot, device(0, 0, wrap_step), 30).wait_recv()
+        when(hands, handed().start)
 
     def open_far():
         pl.semaphore_wait(ready_y, 1)
@@ -390,50 +415,102 @@
             when(far[step], lambda: start(along_y(step)))
 
     for step in steps:
-        when(jnp.logical_not(both(far[step], late)), lambda: start(along_y(step)))
+        when(jnp.logical_not(far[step] & (ends | both(sided_y, late))) | (far[step] & pushes), lambda: start(along_y(step)))
     when(corner & late, lambda: start(corners()))
     send_early(0)
     for cy in (1, 2):
         when(jnp.logical_not(from_far[cy]), lambda: pass_near(cy))
-    when(wrap[-1], open_wrap)
+    when(hold, open_wrap)
     when(both(corner, late), open_corner)
-    when(both(far_any, late), open_far)
+    when(corner, forward_corner)
+    for step in steps:
+        when(wrap[-step], lambda: pass_wrap(0, step))
+        for cy in (1, 2):
+            when(both(wrap[-step], from_far[cy]), lambda: pass_wrap(cy, step))
+    when(both(direct & sided_y, late), open_far)
     for cy in (1, 2):
         when(from_far[cy], lambda: pass_far(cy))
     for cy in range(3):
-        for copy in along_x(cy) + fan(cy, 1) + fan(cy, -1):
+        for copy in along_x(cy):
             copy.wait_recv()
+        for step in steps:
+            copies = fan(cy, step)
+            when(jnp.logical_not(wrap[-step]), copies[0].wait_recv)
+            for copy in copies[1:]:
+                copy.wait_recv()
     for step in steps:
-        finish(along_y(step))
+        when(jnp.logical_not(far[step] & ends) | (far[step] & pushes), lambda: finish(along_y(step)))
     for cy in range(3):
         finish(along_x(cy))
         for step in steps:
+            when(jnp.logical_not(wrap[step]), lambda: finish(fan(cy, step)[1:]))
             if cy == 0:
-                finish(fan(cy, step))
+                finish(fan(cy, step)[:1])
+                when(wrap[-step], lambda: finish(onward(cy, step)))
             else:
-                when(jnp.logical_not(from_far[cy] & wrap[step]), lambda: finish(fan(cy, step)))
+                when(jnp.logical_not(from_far[cy] & wrap[step]), lambda: finish(fan(cy, step)[:1]))
+                when(both(wrap[-step], from_far[cy]), lambda: finish(onward(cy, step)))
     when(corner, lambda: finish(corners()))
-    for n in range(27):
-        meta_out[pl.ds(n, 1), :] = atoms_out[n, pl.ds(32, 1), :].astype(jnp.int32)
-
-def exchange(positions, charges, block_anchor, block_atoms, brick_blocks):
-    smem = pl.BlockSpec(memory_space=pltpu.SMEM)
+    when(hands, lambda: finish([handed()]))
+    for a in range(3):
+        atoms_out[SOURCES, pl.ds(a, 1), :] = jnp.full((1, LANES), scale_ref[a], jnp.float32)
+    rows_ref[...] = jnp.zeros_like(rows_ref)
+    for n in range(SOURCES):
+        rows_ref[pl.ds(n, 1), :] = atoms_out[n, pl.ds(32, 1), :]
+    value = rows_ref[...].astype(jnp.int32)
+    source = lax.broadcasted_iota(jnp.int32, value.shape, 0)
+    place = lax.broadcasted_iota(jnp.int32, value.shape, 1)
+    one = jnp.ones_like(value)
+    zero = jnp.zeros_like(value)
+    cx = jnp.where(source >= 9, one, zero) + jnp.where(source >= 18, one, zero)
+    rest = source - 9 * cx
+    cz = jnp.where(rest >= 3, one, zero) + jnp.where(rest >= 6, one, zero)
+    cy = rest - 3 * cz
+    is_z = (place >= 2 * BLOCKS) & (place < 3 * BLOCKS)
+    is_live = place >= 3 * BLOCKS
+    kind = jnp.where(place < BLOCKS, cx, jnp.where(place < 2 * BLOCKS, cy, cz))
+    period = jnp.where(is_z, CZ, CX)
+    low = jnp.where(is_live, 1, jnp.where(kind == 1, jnp.where(is_z, CZ - 19, 5), 0))
+    high = jnp.where(jnp.logical_not(is_live) & (kind == 2), 11, 999)
+    fits = jnp.where((value >= low) & (value <= high), one, zero)
+    used = fits
+    for group in (1, 2, 3):
+        used = used * pltpu.roll(fits, LANES - group * BLOCKS, 1)
+    used = pltpu.roll(used, 4 * BLOCKS, 1)
+    shifted = value + jnp.where(is_live | (kind == 0), 0, jnp.where(kind == 1, -period, period))
+    meta_out[...] = jnp.where(place >= 4 * BLOCKS, used, shifted)
+
+
+def exchange(positions, charges, block_anchor, block_atoms, brick_blocks, box_scale):
+    anywhere = pl.BlockSpec(memory_space=pl.ANY)
     vmem = pl.BlockSpec(memory_space=pltpu.VMEM)
+    f32, i32 = jnp.float32, jnp.int32
     return pl.pallas_call(
         exchange_kernel,
-        out_shape=(jax.ShapeDtypeStruct((27, ROWS, 128), jnp.float32), jax.ShapeDtypeStruct((32, 128), jnp.int32)),
-        in_specs=[vmem, vmem, smem, smem, smem],
+        out_shape=(jax.ShapeDtypeStruct((SOURCES + 1, ROWS, LANES), f32), jax.ShapeDtypeStruct((32, LANES), i32)),
+        in_specs=[anywhere] * 6,
         out_specs=(vmem, vmem),
-        scratch_shapes=[pltpu.SemaphoreType.DMA((32,)), pltpu.SemaphoreType.DMA((27,)),
-                        pltpu.SemaphoreType.REGULAR((3,))],
+        scratch_shapes=[
+            pltpu.VMEM((3, BLOCKS * LANES), f32),
+            pltpu.VMEM((BLOCKS, LANES), f32),
+            pltpu.SMEM((3, BLOCKS), i32),
+            pltpu.SMEM((BLOCKS,), i32),
+            pltpu.SMEM((1,), i32),
+            pltpu.SMEM((3,), f32),
+            pltpu.VMEM((32, LANES), f32),
+            pltpu.SemaphoreType.DMA((6,)),
+            pltpu.SemaphoreType.DMA((40,)),
+            pltpu.SemaphoreType.DMA((SOURCES,)),
+            pltpu.SemaphoreType.REGULAR((3,)),
+        ],
         compiler_params=pltpu.CompilerParams(collective_id=0, has_side_effects=True),
         name="exchange_atoms",
-    )(positions, charges.reshape(8, 128), block_anchor, block_atoms, brick_blocks)
+    )(positions, charges.reshape(BLOCKS, LANES), block_anchor, block_atoms, brick_blocks, box_scale)
 
 
 def per_device(positions, charges, block_anchor, block_atoms, brick_blocks, box_scale):
-    atoms, meta = exchange(positions, charges, block_anchor, block_atoms, brick_blocks)
-    potential, forces = make_field(atoms, meta, box_scale)
+    atoms, meta = exchange(positions, charges, block_anchor, block_atoms, brick_blocks, box_scale)
+    potential, forces = make_field(atoms, meta)
     return (potential, forces)
 
 

time: 50.6 us -> 42.2 us (0.83)
  the two profiles are of different devices: /device:TPU:417 before, /device:TPU:1 now
where the time goes in v3:
time: 42.2 us; the launch traced here: 41.9 us
  Pallas kernels  38.8 us (92%)
  local copies, waits for them, and re-layouts  1.77 us (4%)
  between operations  1.29 us (3%)
    pallas_call x1, Pallas kernels, exchange(): pl.pallas_call(exchange_kernel, out_shape=(jax.ShapeDtypeStruct((SOURCES...  26.9 us
    pallas_call x1, Pallas kernels, make_field(): pl.pallas_call(field_kernel, out_shape=(jax.ShapeDtypeStruct((CX, CY, CZ)...  11.9 us
    unnamed x4, local copies, waits for them, and re-layouts  1.77 us

profile of v3, /device:TPU:1, one launch (start us, length us, event | category | flops | bytes accessed | tf_op | source)
XLA Modules:
  0.0 41.9 jit_solution(5577388522655222905)
XLA Ops:
  1.3 26.9 %exchange_atoms.1 = (f32[28,33,128]{2,1,0:T(8,128)}, s32[32,128]{1,0:T(8,128)}) custom-call(f32[3,1024]{1,0:T(4,128)} %pos_in.1, f32[8,128]{1,0:T(8,128)} %bitcast.1, s32[3,8]{1,0:T(4,128)} %anchor_in.1, s32[8]{0:T(128)} %atoms_in.1, s32[1]{0:T(128)S(6)} %copy.8.blocks_in, f32[3]{0:T(128)} %scale_in.1), custom_call_target="tpu_custom_call" | custom-call | tf_op jit(solution)/shard_map/exchange_atoms/pallas_call | solution.py:488
  28.2 0.0 copy-start
  28.2 1.1 %copy-done = f32[28,33,128]{2,1,0:T(8,128)S(1)} copy-done((f32[28,33,128]{2,1,0:T(8,128)S(1)}, f32[28,33,128]{2,1,0:T(8,128)}, u32[]{:S(2)}) %copy-start) | copy-done | bytes 473112
  29.3 0.0 copy-start.1
  29.3 0.7 %copy-done.1 = s32[32,128]{1,0:T(8,128)S(1)} copy-done((s32[32,128]{1,0:T(8,128)S(1)}, s32[32,128]{1,0:T(8,128)}, u32[]{:S(2)}) %copy-start.1) | copy-done | bytes 16408
  30.0 11.9 %field_and_forces.1 = (f32[24,24,128]{2,1,0:T(8,128)}, f32[3,1024]{1,0:T(4,128)}) custom-call(s32[32,128]{1,0:T(8,128)S(1)} %copy-done.1, f32[28,33,128]{2,1,0:T(8,128)S(1)} %copy-done), custom_call_target="tpu_custom_call" | custom-call | tf_op jit(solution)/shard_map/field_and_forces/pallas_call | solution.py:213
Async XLA Ops:
  28.2 1.1 %copy-start = (f32[28,33,128]{2,1,0:T(8,128)S(1)}, f32[28,33,128]{2,1,0:T(8,128)}, u32[]{:S(2)}) copy-start(f32[28,33,128]{2,1,0:T(8,128)} %get-tuple-element.5.atoms_in) | copy-start | bytes 1419268
  29.3 0.7 %copy-start.1 = (s32[32,128]{1,0:T(8,128)S(1)}, s32[32,128]{1,0:T(8,128)}, u32[]{:S(2)}) copy-start(s32[32,128]{1,0:T(8,128)} %get-tuple-element.4.meta_in) | copy-start | bytes 49156

commit v4 on v3

--- a/solution.py
+++ b/solution.py
@@ -231,7 +231,7 @@
             pltpu.VMEM((4 * Z_ROWS, 256), f32),
             pltpu.VMEM((SPAN, SPAN, 4 * LANES), jnp.bfloat16),
         ],
-        compiler_params=pltpu.CompilerParams(vmem_limit_bytes=40 * 1024 * 1024),
+        compiler_params=pltpu.CompilerParams(vmem_limit_bytes=60 * 1024 * 1024),
         name="field_and_forces",
     )(meta, atoms)
 

time: 42.2 us -> 42 us (level)
  local copies, waits for them, and re-layouts: 1.77 us -> 0 us
  Pallas kernels: 38.8 us -> 40.4 us
    unnamed x4 -> x0, local copies, waits for them, and re-layouts: 1.77 us -> none
    pallas_call x1, Pallas kernels: 11.9 us -> 13.5 us  [make_field(): pl.pallas_call(field_kernel, out_shape=(jax.ShapeDtypeStruct((CX, CY, CZ)...]
where the time goes in v4:
time: 42 us; the launch traced here: 41.7 us
  Pallas kernels  40.4 us (96%)
  between operations  1.29 us (3%)
    pallas_call x1, Pallas kernels, exchange(): pl.pallas_call(exchange_kernel, out_shape=(jax.ShapeDtypeStruct((SOURCES...  27 us
    pallas_call x1, Pallas kernels, make_field(): pl.pallas_call(field_kernel, out_shape=(jax.ShapeDtypeStruct((CX, CY, CZ)...  13.5 us

profile of v4, /device:TPU:1, one launch (start us, length us, event | category | flops | bytes accessed | tf_op | source)
XLA Modules:
  0.0 41.7 jit_solution(2347819253197775589)
XLA Ops:
  1.3 27.0 %exchange_atoms.1 = (f32[28,33,128]{2,1,0:T(8,128)}, s32[32,128]{1,0:T(8,128)}) custom-call(f32[3,1024]{1,0:T(4,128)} %pos_in.1, f32[8,128]{1,0:T(8,128)} %bitcast.1, s32[3,8]{1,0:T(4,128)} %anchor_in.1, s32[8]{0:T(128)} %atoms_in.1, s32[1]{0:T(128)S(6)} %copy.8.blocks_in, f32[3]{0:T(128)} %scale_in.1), custom_call_target="tpu_custom_call" | custom-call | tf_op jit(solution)/shard_map/exchange_atoms/pallas_call | solution.py:488
  28.2 13.5 %field_and_forces.1 = (f32[24,24,128]{2,1,0:T(8,128)}, f32[3,1024]{1,0:T(4,128)}) custom-call(s32[32,128]{1,0:T(8,128)} %get-tuple-element.4.meta_in, f32[28,33,128]{2,1,0:T(8,128)} %get-tuple-element.5.atoms_in), custom_call_target="tpu_custom_call" | custom-call | tf_op jit(solution)/shard_map/field_and_forces/pallas_call | solution.py:213

commit v5 on v4

--- a/solution.py
+++ b/solution.py
@@ -27,6 +27,7 @@
 WAYS = 16
 EMPTY = SLOTS + WAYS
 PAD = 40
+LENGTH = CZ + 2 * (RIM + RADIUS)
 
 
 def norm(width):
@@ -46,13 +47,27 @@
     return high, (value - high.astype(jnp.float32)).astype(jnp.bfloat16)
 
 
-def field_kernel(meta_in, atoms_in, potential, forces, meta, atoms, load_sems, order, tasks, starts, pad_x, pad_y, pad_z, wx_all, wy_all, wz_all, density, field):
+def kernel_taps(scales):
+    taps = []
+    for scale in scales:
+        tau = SMOOTH * scale
+        taps.append([jnp.exp(-float(e * e) / (2.0 * tau * tau)) * norm(tau) for e in range(RADIUS + 1)])
+    return taps
+
+
+def field_kernel(meta_in, atoms_in, own_in, potential, forces, meta, atoms, load_sems, order, tasks, starts, pad_x, pad_y, pad_z, wx_all, wy_all, wz_all, density, field):
     f32 = jnp.float32
     load_meta = pltpu.make_async_copy(meta_in, meta, load_sems.at[0])
     load_meta.start()
     load_atoms = pltpu.make_async_copy(atoms_in, atoms, load_sems.at[1])
     load_atoms.start()
-    density[...] = jnp.zeros_like(density)
+    load_own = []
+    for quarter in range(4):
+        load_own.append(pltpu.make_async_copy(own_in.at[quarter], density.at[pl.ds(quarter * Z_ROWS + 16, LENGTH)], load_sems.at[2 + quarter]))
+        load_own[-1].start()
+    for quarter in range(4):
+        for first in (0, 16 + LENGTH):
+            density[pl.ds(quarter * Z_ROWS + first, 16), :] = jnp.zeros((16, 256), f32)
     for ref in (pad_x, pad_y, pad_z):
         ref[...] = jnp.zeros_like(ref)
     wx_all[pl.ds(EMPTY * SPAN, SPAN), :] = jnp.zeros((SPAN, LANES), f32)
@@ -67,16 +82,13 @@
             count = count + meta[n, 4 * BLOCKS + b]
         return count
 
-    blocks = lax.fori_loop(0, SOURCES, choose, jnp.int32(0))
+    blocks = lax.fori_loop(1, SOURCES, choose, jnp.int32(0))
     for extra in range(WAYS - 1):
         order[blocks + extra] = 0
     load_atoms.wait()
     scales = [atoms[SOURCES, pl.ds(a, 1), :] for a in range(3)]
     widths = [SPREAD * s for s in scales]
-    taps = []
-    for a in range(3):
-        tau = SMOOTH * scales[a]
-        taps.append([jnp.exp(-float(e * e) / (2.0 * tau * tau)) * norm(tau) for e in range(RADIUS + 1)])
+    taps = kernel_taps(scales)
 
     iota16 = lax.broadcasted_iota(jnp.int32, (PATCH, LANES), 0)
 
@@ -120,6 +132,9 @@
     for extra in range(WAYS - 1):
         tasks[jobs + extra] = EMPTY * 4
 
+    for load in load_own:
+        load.wait()
+
     def spread(group, carry):
         for way in range(WAYS):
             code = tasks[group * WAYS + way]
@@ -142,7 +157,7 @@
 
     lax.fori_loop(0, (jobs + WAYS - 1) // WAYS, spread, jnp.int32(0))
 
-    length = CZ + 2 * (RIM + RADIUS)
+    length = LENGTH
     gap = lax.broadcasted_iota(jnp.int32, (length, length), 0) - lax.broadcasted_iota(jnp.int32, (length, length), 1)
     gap_f = gap.astype(f32)
     tau_v = jnp.broadcast_to(SMOOTH * scales[2][:, :1], (length, length))
@@ -206,19 +221,19 @@
         force(b)
 
 
-def make_field(atoms, meta):
+def make_field(atoms, meta, own):
     anywhere = pl.BlockSpec(memory_space=pl.ANY)
     vmem = pl.BlockSpec(memory_space=pltpu.VMEM)
     f32, i32 = jnp.float32, jnp.int32
     return pl.pallas_call(
         field_kernel,
         out_shape=(jax.ShapeDtypeStruct((CX, CY, CZ), f32), jax.ShapeDtypeStruct((3, BLOCKS * LANES), f32)),
-        in_specs=[anywhere, anywhere],
+        in_specs=[anywhere, anywhere, anywhere],
         out_specs=(vmem, vmem),
         scratch_shapes=[
             pltpu.SMEM((32, LANES), i32),
             pltpu.VMEM((SOURCES + 1, ROWS, LANES), f32),
-            pltpu.SemaphoreType.DMA((2,)),
+            pltpu.SemaphoreType.DMA((6,)),
             pltpu.SMEM((EMPTY + 1,), i32),
             pltpu.SMEM((SLOTS * 4 + WAYS,), i32),
             pltpu.SMEM((EMPTY + 1,), i32),
@@ -233,10 +248,10 @@
         ],
         compiler_params=pltpu.CompilerParams(vmem_limit_bytes=60 * 1024 * 1024),
         name="field_and_forces",
-    )(meta, atoms)
-
-
-def exchange_kernel(pos_in, q_in, anchor_in, atoms_in, blocks_in, scale_in, atoms_out, meta_out, pos_ref, q_ref, anchor_ref, atoms_ref, blocks_ref, scale_ref, rows_ref, load_sems, send_sems, recv_sems, ready_sems):
+    )(meta, atoms, own)
+
+
+def exchange_kernel(pos_in, q_in, anchor_in, atoms_in, blocks_in, scale_in, atoms_out, meta_out, own_out, pos_ref, q_ref, anchor_ref, atoms_ref, blocks_ref, scale_ref, rows_ref, pad_x, pad_y, pad_z, wx_own, wy_own, wz_own, load_sems, send_sems, recv_sems, ready_sems):
     gx, gy, gz = (lax.axis_index(a) for a in ("gx", "gy", "gz"))
     nx, ny, nz = (lax.axis_size(a) for a in ("gx", "gy", "gz"))
     half = ny // 2
@@ -420,6 +435,7 @@
     send_early(0)
     for cy in (1, 2):
         when(jnp.logical_not(from_far[cy]), lambda: pass_near(cy))
+    spread_own(atoms_out, anchor_ref, scale_ref, pad_x, pad_y, pad_z, wx_own, wy_own, wz_own, own_out)
     when(hold, open_wrap)
     when(both(corner, late), open_corner)
     when(corner, forward_corner)
@@ -481,15 +497,64 @@
     meta_out[...] = jnp.where(place >= 4 * BLOCKS, used, shifted)
 
 
+def spread_own(atoms, anchor, scale_ref, pad_x, pad_y, pad_z, wx_own, wy_own, wz_own, own_out):
+    f32 = jnp.float32
+    scales = [jnp.full((1, LANES), scale_ref[a], f32) for a in range(3)]
+    widths = [SPREAD * s for s in scales]
+    taps = kernel_taps(scales)
+    iota16 = lax.broadcasted_iota(jnp.int32, (PATCH, LANES), 0)
+    for ref in (pad_x, pad_y, pad_z):
+        ref[...] = jnp.zeros_like(ref)
+
+    def weigh(b, carry):
+        x = atoms[0, pl.ds(b, 1), :] * scales[0]
+        y = atoms[0, pl.ds(b + BLOCKS, 1), :] * scales[1]
+        z = atoms[0, pl.ds(b + 2 * BLOCKS, 1), :] * scales[2]
+        q = atoms[0, pl.ds(b + 3 * BLOCKS, 1), :]
+        pad_x[b, pl.ds(PAD, PATCH), :] = q * window(x, iota16, widths[0])[0]
+        pad_y[b, pl.ds(PAD, PATCH), :] = window(y, iota16, widths[1])[0]
+        pad_z[b, pl.ds(LENGTH, PATCH), :] = window(z, iota16, widths[2])[0]
+        for a, pad, out in ((0, pad_x, wx_own), (1, pad_y, wy_own)):
+            start = PAD - anchor[a, b]
+            total = taps[a][0] * pad[b, pl.ds(start, SPAN), :]
+            for e in range(1, RADIUS + 1):
+                total = total + taps[a][e] * (pad[b, pl.ds(start - e, SPAN), :] + pad[b, pl.ds(start + e, SPAN), :])
+            out[b] = total
+        high, low = split(pad_z[b, pl.ds(LENGTH - 4 - anchor[2, b], LENGTH), :])
+        wz_own[b, pl.ds(0, LENGTH), :] = high
+        wz_own[b, pl.ds(LENGTH, LENGTH), :] = low
+        return carry
+
+    lax.fori_loop(0, BLOCKS, weigh, jnp.int32(0))
+
+    def spread(quarter, carry):
+        half = quarter // 2
+        side = quarter % 2
+        left, right = [], []
+        for b in range(BLOCKS):
+            wx = wx_own[b, pl.ds(pl.multiple_of(half * 16, 16), 16), :]
+            wy = wy_own[b, pl.ds(pl.multiple_of(side * 16, 16), 16), :]
+            right += split((wx[:, None, :] * wy[None, :, :]).reshape(256, LANES))
+            left += [wz_own[b]] * 2
+        patch = lax.dot_general(
+            jnp.concatenate(left, axis=1), jnp.concatenate(right, axis=1),
+            (((1,), (1,)), ((), ())), preferred_element_type=f32)
+        own_out[quarter] = patch[:LENGTH] + patch[LENGTH:]
+        return carry
+
+    lax.fori_loop(0, 4, spread, jnp.int32(0))
+
+
 def exchange(positions, charges, block_anchor, block_atoms, brick_blocks, box_scale):
     anywhere = pl.BlockSpec(memory_space=pl.ANY)
     vmem = pl.BlockSpec(memory_space=pltpu.VMEM)
     f32, i32 = jnp.float32, jnp.int32
     return pl.pallas_call(
         exchange_kernel,
-        out_shape=(jax.ShapeDtypeStruct((SOURCES + 1, ROWS, LANES), f32), jax.ShapeDtypeStruct((32, LANES), i32)),
+        out_shape=(jax.ShapeDtypeStruct((SOURCES + 1, ROWS, LANES), f32), jax.ShapeDtypeStruct((32, LANES), i32),
+                   jax.ShapeDtypeStruct((4, LENGTH, 256), f32)),
         in_specs=[anywhere] * 6,
-        out_specs=(vmem, vmem),
+        out_specs=(vmem, vmem, vmem),
         scratch_shapes=[
             pltpu.VMEM((3, BLOCKS * LANES), f32),
             pltpu.VMEM((BLOCKS, LANES), f32),
@@ -498,19 +563,25 @@
             pltpu.SMEM((1,), i32),
             pltpu.SMEM((3,), f32),
             pltpu.VMEM((32, LANES), f32),
+            pltpu.VMEM((BLOCKS, 96, LANES), f32),
+            pltpu.VMEM((BLOCKS, 96, LANES), f32),
+            pltpu.VMEM((BLOCKS, 2 * LENGTH + PATCH, LANES), f32),
+            pltpu.VMEM((BLOCKS, SPAN, LANES), f32),
+            pltpu.VMEM((BLOCKS, SPAN, LANES), f32),
+            pltpu.VMEM((BLOCKS, 2 * LENGTH, LANES), jnp.bfloat16),
             pltpu.SemaphoreType.DMA((6,)),
             pltpu.SemaphoreType.DMA((40,)),
             pltpu.SemaphoreType.DMA((SOURCES,)),
             pltpu.SemaphoreType.REGULAR((3,)),
         ],
-        compiler_params=pltpu.CompilerParams(collective_id=0, has_side_effects=True),
+        compiler_params=pltpu.CompilerParams(collective_id=0, has_side_effects=True, vmem_limit_bytes=60 * 1024 * 1024),
         name="exchange_atoms",
     )(positions, charges.reshape(BLOCKS, LANES), block_anchor, block_atoms, brick_blocks, box_scale)
 
 
 def per_device(positions, charges, block_anchor, block_atoms, brick_blocks, box_scale):
-    atoms, meta = exchange(positions, charges, block_anchor, block_atoms, brick_blocks, box_scale)
-    potential, forces = make_field(atoms, meta)
+    atoms, meta, own = exchange(positions, charges, block_anchor, block_atoms, brick_blocks, box_scale)
+    potential, forces = make_field(atoms, meta, own)
     return (potential, forces)
 
 

time: 42 us -> 39.5 us (0.940)
  the two profiles are of different devices: /device:TPU:1 before, /device:TPU:3 now
where the time goes in v5:
time: 39.5 us; the launch traced here: 39.2 us
  Pallas kernels  37.9 us (96%)
  between operations  1.29 us (3%)
    pallas_call x1, Pallas kernels, exchange(): pl.pallas_call(exchange_kernel, out_shape=(jax.ShapeDtypeStruct((SOURCES...  25.9 us
    pallas_call x1, Pallas kernels, make_field(): pl.pallas_call(field_kernel, out_shape=(jax.ShapeDtypeStruct((CX, CY, CZ)...  12 us

profile of v5, /device:TPU:3, one launch (start us, length us, event | category | flops | bytes accessed | tf_op | source)
XLA Modules:
  0.0 39.2 jit_solution(16193775501929454450)
XLA Ops:
  1.3 25.9 %exchange_atoms.1 = (f32[28,33,128]{2,1,0:T(8,128)}, s32[32,128]{1,0:T(8,128)}, f32[4,144,256]{2,1,0:T(8,128)}) custom-call(f32[3,1024]{1,0:T(4,128)} %pos_in.1, f32[8,128]{1,0:T(8,128)} %bitcast.1, s32[3,8]{1,0:T(4,128)} %anchor_in.1, s32[8]{0:T(128)} %atoms_in.1, s32[1]{0:T(128)S(6)} %copy.8.blocks_in, f32[3]{0:T(128)} %scale_in.1), custom_call_target="tpu_custom_call" | custom-call | tf_op jit(solution)/shard_map/exchange_atoms/pallas_call | solution.py:552
  27.2 12.0 %field_and_forces.1 = (f32[24,24,128]{2,1,0:T(8,128)}, f32[3,1024]{1,0:T(4,128)}) custom-call(s32[32,128]{1,0:T(8,128)} %get-tuple-element.5.meta_in, f32[28,33,128]{2,1,0:T(8,128)} %get-tuple-element.6.atoms_in, f32[4,144,256]{2,1,0:T(8,128)} %get-tuple-element.7.own_in), custom_call_target="tpu_custom_call" | custom-call | tf_op jit(solution)/shard_map/field_and_forces/pallas_call | solution.py:228

commit v6 on v5

--- a/solution.py
+++ b/solution.py
@@ -55,16 +55,14 @@
     return taps
 
 
-def field_kernel(meta_in, atoms_in, own_in, potential, forces, meta, atoms, load_sems, order, tasks, starts, pad_x, pad_y, pad_z, wx_all, wy_all, wz_all, density, field):
+def field_kernel(meta_in, atoms, near_in, rights, potential, forces, meta, load_sems, order, tasks, starts, pad_x, pad_y, pad_z, wx_all, wy_all, wz_all, density, field):
     f32 = jnp.float32
     load_meta = pltpu.make_async_copy(meta_in, meta, load_sems.at[0])
     load_meta.start()
-    load_atoms = pltpu.make_async_copy(atoms_in, atoms, load_sems.at[1])
-    load_atoms.start()
-    load_own = []
+    load_near = []
     for quarter in range(4):
-        load_own.append(pltpu.make_async_copy(own_in.at[quarter], density.at[pl.ds(quarter * Z_ROWS + 16, LENGTH)], load_sems.at[2 + quarter]))
-        load_own[-1].start()
+        load_near.append(pltpu.make_async_copy(near_in.at[quarter], density.at[pl.ds(quarter * Z_ROWS + 16, LENGTH)], load_sems.at[1 + quarter]))
+        load_near[-1].start()
     for quarter in range(4):
         for first in (0, 16 + LENGTH):
             density[pl.ds(quarter * Z_ROWS + first, 16), :] = jnp.zeros((16, 256), f32)
@@ -85,7 +83,6 @@
     blocks = lax.fori_loop(1, SOURCES, choose, jnp.int32(0))
     for extra in range(WAYS - 1):
         order[blocks + extra] = 0
-    load_atoms.wait()
     scales = [atoms[SOURCES, pl.ds(a, 1), :] for a in range(3)]
     widths = [SPREAD * s for s in scales]
     taps = kernel_taps(scales)
@@ -132,7 +129,7 @@
     for extra in range(WAYS - 1):
         tasks[jobs + extra] = EMPTY * 4
 
-    for load in load_own:
+    for load in load_near:
         load.wait()
 
     def spread(group, carry):
@@ -183,29 +180,16 @@
                 field[place[0], place[1], pl.ds(i * LANES, LANES)] = block.reshape(16, 16, LANES)
 
     iota32 = lax.broadcasted_iota(jnp.int32, (SPAN, LANES), 0)
-    iota_z = lax.broadcasted_iota(jnp.int32, (CZ, LANES), 0)
-    iota8 = lax.broadcasted_iota(jnp.int32, (8, LANES), 0)
-    edge_z = jnp.where(iota8 < 4, iota8 - 4, iota8 + (CZ - 4))
-
     def force(b):
         x = atoms[0, pl.ds(b, 1), :] * scales[0]
         y = atoms[0, pl.ds(b + BLOCKS, 1), :] * scales[1]
-        z = atoms[0, pl.ds(b + 2 * BLOCKS, 1), :] * scales[2]
         q = atoms[0, pl.ds(b + 3 * BLOCKS, 1), :]
         at_x = meta[0, b]
         at_y = meta[0, BLOCKS + b]
-        at_z = meta[0, 2 * BLOCKS + b]
         wx, sx = window(x, iota16, widths[0])
         wy, sy = window(y, iota32 - at_y, widths[1])
-        wz, sz = window(z, iota_z - at_z + RIM, widths[2])
-        we, se = window(z, edge_z - at_z + RIM, widths[2])
-        main_high, main_low = split(jnp.concatenate([wz, sz], axis=1))
-        rim = jnp.concatenate([we, se], axis=1)
-        rim_high = rim.astype(jnp.bfloat16).astype(f32)
-        rim = jnp.concatenate([rim_high, rim_high, rim - rim_high, jnp.zeros((LANES - 24, 256), f32)], axis=0).astype(jnp.bfloat16)
-        right = jnp.concatenate([main_high, main_high, main_low, rim], axis=0)
         left = field[pl.ds(at_x, PATCH)].reshape(PATCH * SPAN, 4 * LANES)
-        values = jnp.dot(left, right, preferred_element_type=f32).reshape(PATCH, SPAN, 256)
+        values = jnp.dot(left, rights[b], preferred_element_type=f32).reshape(PATCH, SPAN, 256)
         by_sx = jnp.zeros((SPAN, LANES), f32)
         by_wx = jnp.zeros((SPAN, LANES), f32)
         by_wz = jnp.zeros((SPAN, LANES), f32)
@@ -221,19 +205,18 @@
         force(b)
 
 
-def make_field(atoms, meta, own):
+def make_field(atoms, meta, near, rights):
     anywhere = pl.BlockSpec(memory_space=pl.ANY)
     vmem = pl.BlockSpec(memory_space=pltpu.VMEM)
     f32, i32 = jnp.float32, jnp.int32
     return pl.pallas_call(
         field_kernel,
         out_shape=(jax.ShapeDtypeStruct((CX, CY, CZ), f32), jax.ShapeDtypeStruct((3, BLOCKS * LANES), f32)),
-        in_specs=[anywhere, anywhere, anywhere],
+        in_specs=[anywhere, vmem, anywhere, vmem],
         out_specs=(vmem, vmem),
         scratch_shapes=[
             pltpu.SMEM((32, LANES), i32),
-            pltpu.VMEM((SOURCES + 1, ROWS, LANES), f32),
-            pltpu.SemaphoreType.DMA((6,)),
+            pltpu.SemaphoreType.DMA((5,)),
             pltpu.SMEM((EMPTY + 1,), i32),
             pltpu.SMEM((SLOTS * 4 + WAYS,), i32),
             pltpu.SMEM((EMPTY + 1,), i32),
@@ -246,12 +229,12 @@
             pltpu.VMEM((4 * Z_ROWS, 256), f32),
             pltpu.VMEM((SPAN, SPAN, 4 * LANES), jnp.bfloat16),
         ],
-        compiler_params=pltpu.CompilerParams(vmem_limit_bytes=60 * 1024 * 1024),
+        compiler_params=pltpu.CompilerParams(vmem_limit_bytes=24 * 1024 * 1024),
         name="field_and_forces",
-    )(meta, atoms, own)
-
-
-def exchange_kernel(pos_in, q_in, anchor_in, atoms_in, blocks_in, scale_in, atoms_out, meta_out, own_out, pos_ref, q_ref, anchor_ref, atoms_ref, blocks_ref, scale_ref, rows_ref, pad_x, pad_y, pad_z, wx_own, wy_own, wz_own, load_sems, send_sems, recv_sems, ready_sems):
+    )(meta, atoms, near, rights)
+
+
+def exchange_kernel(pos_in, q_in, anchor_in, atoms_in, blocks_in, scale_in, atoms_out, meta_out, near_out, right_out, pos_ref, q_ref, anchor_ref, atoms_ref, blocks_ref, scale_ref, rows_ref, pad_x, pad_y, pad_z, wx_near, wy_near, wz_near, near_sum, rights, load_sems, send_sems, recv_sems, ready_sems):
     gx, gy, gz = (lax.axis_index(a) for a in ("gx", "gy", "gz"))
     nx, ny, nz = (lax.axis_size(a) for a in ("gx", "gy", "gz"))
     half = ny // 2
@@ -435,7 +418,13 @@
     send_early(0)
     for cy in (1, 2):
         when(jnp.logical_not(from_far[cy]), lambda: pass_near(cy))
-    spread_own(atoms_out, anchor_ref, scale_ref, pad_x, pad_y, pad_z, wx_own, wy_own, wz_own, own_out)
+    scales = [jnp.full((1, LANES), scale_ref[a], jnp.float32) for a in range(3)]
+    weigh_own(scales, atoms_out, anchor_ref, pad_x, pad_y, pad_z, wx_near, wy_near, wz_near, rights)
+    store_rights = pltpu.make_async_copy(rights, right_out, load_sems.at[6])
+    store_rights.start()
+    spread_near(wx_near, wy_near, wz_near, near_sum)
+    store_near = pltpu.make_async_copy(near_sum, near_out, load_sems.at[7])
+    store_near.start()
     when(hold, open_wrap)
     when(both(corner, late), open_corner)
     when(corner, forward_corner)
@@ -470,6 +459,8 @@
     when(hands, lambda: finish([handed()]))
     for a in range(3):
         atoms_out[SOURCES, pl.ds(a, 1), :] = jnp.full((1, LANES), scale_ref[a], jnp.float32)
+    store_rights.wait()
+    store_near.wait()
     rows_ref[...] = jnp.zeros_like(rows_ref)
     for n in range(SOURCES):
         rows_ref[pl.ds(n, 1), :] = atoms_out[n, pl.ds(32, 1), :]
@@ -497,12 +488,14 @@
     meta_out[...] = jnp.where(place >= 4 * BLOCKS, used, shifted)
 
 
-def spread_own(atoms, anchor, scale_ref, pad_x, pad_y, pad_z, wx_own, wy_own, wz_own, own_out):
+def weigh_own(scales, atoms, anchor, pad_x, pad_y, pad_z, wx_near, wy_near, wz_near, rights):
     f32 = jnp.float32
-    scales = [jnp.full((1, LANES), scale_ref[a], f32) for a in range(3)]
     widths = [SPREAD * s for s in scales]
     taps = kernel_taps(scales)
     iota16 = lax.broadcasted_iota(jnp.int32, (PATCH, LANES), 0)
+    iota_z = lax.broadcasted_iota(jnp.int32, (CZ, LANES), 0)
+    iota8 = lax.broadcasted_iota(jnp.int32, (8, LANES), 0)
+    edge_z = jnp.where(iota8 < 4, iota8 - 4, iota8 + (CZ - 4))
     for ref in (pad_x, pad_y, pad_z):
         ref[...] = jnp.zeros_like(ref)
 
@@ -514,32 +507,42 @@
         pad_x[b, pl.ds(PAD, PATCH), :] = q * window(x, iota16, widths[0])[0]
         pad_y[b, pl.ds(PAD, PATCH), :] = window(y, iota16, widths[1])[0]
         pad_z[b, pl.ds(LENGTH, PATCH), :] = window(z, iota16, widths[2])[0]
-        for a, pad, out in ((0, pad_x, wx_own), (1, pad_y, wy_own)):
+        for a, pad, out in ((0, pad_x, wx_near), (1, pad_y, wy_near)):
             start = PAD - anchor[a, b]
             total = taps[a][0] * pad[b, pl.ds(start, SPAN), :]
             for e in range(1, RADIUS + 1):
                 total = total + taps[a][e] * (pad[b, pl.ds(start - e, SPAN), :] + pad[b, pl.ds(start + e, SPAN), :])
             out[b] = total
         high, low = split(pad_z[b, pl.ds(LENGTH - 4 - anchor[2, b], LENGTH), :])
-        wz_own[b, pl.ds(0, LENGTH), :] = high
-        wz_own[b, pl.ds(LENGTH, LENGTH), :] = low
+        wz_near[b, pl.ds(0, LENGTH), :] = high
+        wz_near[b, pl.ds(LENGTH, LENGTH), :] = low
+        wz, sz = window(z, iota_z - anchor[2, b] + RIM, widths[2])
+        we, se = window(z, edge_z - anchor[2, b] + RIM, widths[2])
+        main_high, main_low = split(jnp.concatenate([wz, sz], axis=1))
+        rim = jnp.concatenate([we, se], axis=1)
+        rim_high = rim.astype(jnp.bfloat16).astype(f32)
+        rim = jnp.concatenate([rim_high, rim_high, rim - rim_high, jnp.zeros((LANES - 24, 256), f32)], axis=0)
+        for i, part in enumerate((main_high, main_high, main_low, rim.astype(jnp.bfloat16))):
+            rights[b, pl.ds(i * LANES, LANES), :] = part
         return carry
 
     lax.fori_loop(0, BLOCKS, weigh, jnp.int32(0))
 
+
+def spread_near(wx_near, wy_near, wz_near, near_sum):
     def spread(quarter, carry):
         half = quarter // 2
         side = quarter % 2
         left, right = [], []
-        for b in range(BLOCKS):
-            wx = wx_own[b, pl.ds(pl.multiple_of(half * 16, 16), 16), :]
-            wy = wy_own[b, pl.ds(pl.multiple_of(side * 16, 16), 16), :]
+        for k in range(BLOCKS):
+            wx = wx_near[k, pl.ds(pl.multiple_of(half * 16, 16), 16), :]
+            wy = wy_near[k, pl.ds(pl.multiple_of(side * 16, 16), 16), :]
             right += split((wx[:, None, :] * wy[None, :, :]).reshape(256, LANES))
-            left += [wz_own[b]] * 2
+            left += [wz_near[k]] * 2
         patch = lax.dot_general(
             jnp.concatenate(left, axis=1), jnp.concatenate(right, axis=1),
-            (((1,), (1,)), ((), ())), preferred_element_type=f32)
-        own_out[quarter] = patch[:LENGTH] + patch[LENGTH:]
+            (((1,), (1,)), ((), ())), preferred_element_type=jnp.float32)
+        near_sum[quarter] = patch[:LENGTH] + patch[LENGTH:]
         return carry
 
     lax.fori_loop(0, 4, spread, jnp.int32(0))
@@ -551,10 +554,11 @@
     f32, i32 = jnp.float32, jnp.int32
     return pl.pallas_call(
         exchange_kernel,
-        out_shape=(jax.ShapeDtypeStruct((SOURCES + 1, ROWS, LANES), f32), jax.ShapeDtypeStruct((32, LANES), i32),
-                   jax.ShapeDtypeStruct((4, LENGTH, 256), f32)),
+        out_shape=(pltpu.VMEM((SOURCES + 1, ROWS, LANES), f32), pltpu.VMEM((32, LANES), i32),
+                   pltpu.VMEM((4, LENGTH, 256), f32),
+                   pltpu.VMEM((BLOCKS, 4 * LANES, 256), jnp.bfloat16)),
         in_specs=[anywhere] * 6,
-        out_specs=(vmem, vmem, vmem),
+        out_specs=(vmem, vmem, anywhere, anywhere),
         scratch_shapes=[
             pltpu.VMEM((3, BLOCKS * LANES), f32),
             pltpu.VMEM((BLOCKS, LANES), f32),
@@ -569,7 +573,9 @@
             pltpu.VMEM((BLOCKS, SPAN, LANES), f32),
             pltpu.VMEM((BLOCKS, SPAN, LANES), f32),
             pltpu.VMEM((BLOCKS, 2 * LENGTH, LANES), jnp.bfloat16),
-            pltpu.SemaphoreType.DMA((6,)),
+            pltpu.VMEM((4, LENGTH, 256), f32),
+            pltpu.VMEM((BLOCKS, 4 * LANES, 256), jnp.bfloat16),
+            pltpu.SemaphoreType.DMA((8,)),
             pltpu.SemaphoreType.DMA((40,)),
             pltpu.SemaphoreType.DMA((SOURCES,)),
             pltpu.SemaphoreType.REGULAR((3,)),
@@ -580,8 +586,8 @@
 
 
 def per_device(positions, charges, block_anchor, block_atoms, brick_blocks, box_scale):
-    atoms, meta, own = exchange(positions, charges, block_anchor, block_atoms, brick_blocks, box_scale)
-    potential, forces = make_field(atoms, meta, own)
+    atoms, meta, near, rights = exchange(positions, charges, block_anchor, block_atoms, brick_blocks, box_scale)
+    potential, forces = make_field(atoms, meta, near, rights)
     return (potential, forces)
 
 

time: 39.5 us -> 38.1 us (0.965)
  the two profiles are of different devices: /device:TPU:3 before, /device:TPU:1 now
where the time goes in v6:
time: 38.1 us; the launch traced here: 37.9 us
  Pallas kernels  36.6 us (96%)
  between operations  1.29 us (3%)
    pallas_call x1, Pallas kernels, exchange(): pl.pallas_call(exchange_kernel, out_shape=(pltpu.VMEM((SOURCES + 1, ROWS,...  26.2 us
    pallas_call x1, Pallas kernels, make_field(): pl.pallas_call(field_kernel, out_shape=(jax.ShapeDtypeStruct((CX, CY, CZ)...  10.4 us

profile of v6, /device:TPU:1, one launch (start us, length us, event | category | flops | bytes accessed | tf_op | source)
XLA Modules:
  0.0 37.9 jit_solution(275709622158572524)
XLA Ops:
  1.3 26.2 %exchange_atoms.1 = (f32[28,33,128]{2,1,0:T(8,128)S(1)}, s32[32,128]{1,0:T(8,128)S(1)}, f32[4,144,256]{2,1,0:T(8,128)S(1)}, bf16[8,512,256]{2,1,0:T(8,128)(2,1)S(1)}) custom-call(f32[3,1024]{1,0:T(4,128)} %pos_in.1, f32[8,128]{1,0:T(8,128)} %bitcast.1, s32[3,8]{1,0:T(4,128)} %anchor_in.1, s32[8]{0:T(128)} %atoms_in.1, s32[1]{0:T(128)S(6)} %copy.8.blocks_in, ...), custom_call_target="tpu_custom_call" | custom-call | tf_op jit(solution)/shard_map/exchange_atoms/pallas_call | solution.py:555
  27.5 10.4 %field_and_forces.1 = (f32[24,24,128]{2,1,0:T(8,128)}, f32[3,1024]{1,0:T(4,128)}) custom-call(s32[32,128]{1,0:T(8,128)S(1)} %get-tuple-element.6.meta_in, f32[28,33,128]{2,1,0:T(8,128)S(1)} %get-tuple-element.7.atoms, f32[4,144,256]{2,1,0:T(8,128)S(1)} %get-tuple-element.8.near_in, bf16[8,512,256]{2,1,0:T(8,128)(2,1)S(1)} %get-tuple-element.9.rights), custom_call_target="tpu_custom_call" | custom-call | tf_op jit(solution)/shard_map/field_and_forces/pallas_call | solution.py:212

commit v7 on v6

--- a/solution.py
+++ b/solution.py
@@ -234,7 +234,7 @@
     )(meta, atoms, near, rights)
 
 
-def exchange_kernel(pos_in, q_in, anchor_in, atoms_in, blocks_in, scale_in, atoms_out, meta_out, near_out, right_out, pos_ref, q_ref, anchor_ref, atoms_ref, blocks_ref, scale_ref, rows_ref, pad_x, pad_y, pad_z, wx_near, wy_near, wz_near, near_sum, rights, load_sems, send_sems, recv_sems, ready_sems):
+def exchange_kernel(pos_in, q_in, anchor_in, atoms_in, blocks_in, scale_in, atoms_out, meta_out, near_out, right_out, pos_ref, q_ref, anchor_ref, atoms_ref, blocks_ref, scale_ref, rows_ref, pad_x, pad_y, pad_z, cell_x, cell_y, wx_near, wy_near, wz_near, near_sum, rights, load_sems, send_sems, recv_sems, ready_sems):
     gx, gy, gz = (lax.axis_index(a) for a in ("gx", "gy", "gz"))
     nx, ny, nz = (lax.axis_size(a) for a in ("gx", "gy", "gz"))
     half = ny // 2
@@ -422,7 +422,16 @@
     weigh_own(scales, atoms_out, anchor_ref, pad_x, pad_y, pad_z, wx_near, wy_near, wz_near, rights)
     store_rights = pltpu.make_async_copy(rights, right_out, load_sems.at[6])
     store_rights.start()
-    spread_near(wx_near, wy_near, wz_near, near_sum)
+    beside = both(far_any & sided_y, late)
+
+    def spread_beside():
+        for copy in along_x(0):
+            copy.wait_recv()
+        weigh_beside(scales, atoms_out, cell_x, cell_y, wx_near, wy_near, wz_near)
+        spread_near(2 * BLOCKS, wx_near, wy_near, wz_near, near_sum)
+
+    when(beside, spread_beside)
+    when(jnp.logical_not(beside), lambda: spread_near(BLOCKS, wx_near, wy_near, wz_near, near_sum))
     store_near = pltpu.make_async_copy(near_sum, near_out, load_sems.at[7])
     store_near.start()
     when(hold, open_wrap)
@@ -437,7 +446,10 @@
         when(from_far[cy], lambda: pass_far(cy))
     for cy in range(3):
         for copy in along_x(cy):
-            copy.wait_recv()
+            if cy:
+                copy.wait_recv()
+            else:
+                when(jnp.logical_not(beside), copy.wait_recv)
         for step in steps:
             copies = fan(cy, step)
             when(jnp.logical_not(wrap[-step]), copies[0].wait_recv)
@@ -483,7 +495,7 @@
     used = fits
     for group in (1, 2, 3):
         used = used * pltpu.roll(fits, LANES - group * BLOCKS, 1)
-    used = pltpu.roll(used, 4 * BLOCKS, 1)
+    used = pltpu.roll(used, 4 * BLOCKS, 1) * jnp.where(rest == 0, 1 - beside.astype(jnp.int32), one)
     shifted = value + jnp.where(is_live | (kind == 0), 0, jnp.where(kind == 1, -period, period))
     meta_out[...] = jnp.where(place >= 4 * BLOCKS, used, shifted)
 
@@ -529,12 +541,49 @@
     lax.fori_loop(0, BLOCKS, weigh, jnp.int32(0))
 
 
-def spread_near(wx_near, wy_near, wz_near, near_sum):
+def weigh_beside(scales, atoms, cell_x, cell_y, wx_near, wy_near, wz_near):
+    i32 = jnp.int32
+    widths = [SPREAD * s for s in scales]
+    taps = kernel_taps(scales)
+    iota_x = lax.broadcasted_iota(i32, (24, LANES), 0)
+    iota_y = lax.broadcasted_iota(i32, (40, LANES), 0)
+    iota_z = lax.broadcasted_iota(i32, (LENGTH, LANES), 0)
+    lane = lax.broadcasted_iota(i32, (1, LANES), 1)
+
+    def weigh(b, carry):
+        for half in range(2):
+            n = 9 * (1 + half)
+            k = BLOCKS * (1 + half) + b
+            x = atoms[n, pl.ds(b, 1), :] * scales[0]
+            y = atoms[n, pl.ds(b + BLOCKS, 1), :] * scales[1]
+            z = atoms[n, pl.ds(b + 2 * BLOCKS, 1), :] * scales[2]
+            q = atoms[n, pl.ds(b + 3 * BLOCKS, 1), :]
+            row = atoms[n, pl.ds(32, 1), :]
+            at = [jnp.sum(jnp.where(lane == a * BLOCKS + b, row, 0.0), axis=1, keepdims=True) for a in range(3)]
+            at_x, at_y, at_z = [jnp.broadcast_to(v, (1, LANES)).astype(i32) for v in at]
+            at_x = at_x + (CX if half else -CX)
+            cell_x[half] = q * window(x, iota_x + (half * 16 - 4) - at_x, widths[0])[0]
+            cell_y[half] = window(y, iota_y - 4 - at_y, widths[1])[0]
+            for a, cell, out, count, first in ((0, cell_x, wx_near, 16, half * 16), (1, cell_y, wy_near, SPAN, 0)):
+                total = taps[a][0] * cell[half, pl.ds(4, count), :]
+                for e in range(1, RADIUS + 1):
+                    total = total + taps[a][e] * (cell[half, pl.ds(4 - e, count), :] + cell[half, pl.ds(4 + e, count), :])
+                out[k, pl.ds(first, count), :] = total
+            high, low = split(window(z, iota_z - 4 - at_z, widths[2])[0])
+            wz_near[k, pl.ds(0, LENGTH), :] = high
+            wz_near[k, pl.ds(LENGTH, LENGTH), :] = low
+        return carry
+
+    lax.fori_loop(0, BLOCKS, weigh, jnp.int32(0))
+
+
+def spread_near(count, wx_near, wy_near, wz_near, near_sum):
     def spread(quarter, carry):
         half = quarter // 2
         side = quarter % 2
         left, right = [], []
-        for k in range(BLOCKS):
+        for b in range(count):
+            k = b if b < BLOCKS else b + BLOCKS * half
             wx = wx_near[k, pl.ds(pl.multiple_of(half * 16, 16), 16), :]
             wy = wy_near[k, pl.ds(pl.multiple_of(side * 16, 16), 16), :]
             right += split((wx[:, None, :] * wy[None, :, :]).reshape(256, LANES))
@@ -570,9 +619,11 @@
             pltpu.VMEM((BLOCKS, 96, LANES), f32),
             pltpu.VMEM((BLOCKS, 96, LANES), f32),
             pltpu.VMEM((BLOCKS, 2 * LENGTH + PATCH, LANES), f32),
-            pltpu.VMEM((BLOCKS, SPAN, LANES), f32),
-            pltpu.VMEM((BLOCKS, SPAN, LANES), f32),
-            pltpu.VMEM((BLOCKS, 2 * LENGTH, LANES), jnp.bfloat16),
+            pltpu.VMEM((2, 24, LANES), f32),
+            pltpu.VMEM((2, 40, LANES), f32),
+            pltpu.VMEM((3 * BLOCKS, SPAN, LANES), f32),
+            pltpu.VMEM((3 * BLOCKS, SPAN, LANES), f32),
+            pltpu.VMEM((3 * BLOCKS, 2 * LENGTH, LANES), jnp.bfloat16),
             pltpu.VMEM((4, LENGTH, 256), f32),
             pltpu.VMEM((BLOCKS, 4 * LANES, 256), jnp.bfloat16),
             pltpu.SemaphoreType.DMA((8,)),

time: 38.1 us -> 37.4 us (0.982)
  Pallas kernels: 36.6 us -> 35.9 us
    pallas_call x1, Pallas kernels: 10.4 us -> 9.66 us  [make_field(): pl.pallas_call(field_kernel, out_shape=(jax.ShapeDtypeStruct((CX, CY, CZ)...]
where the time goes in v7:
time: 37.4 us; the launch traced here: 37.2 us
  Pallas kernels  35.9 us (96%)
  between operations  1.29 us (3%)
    pallas_call x1, Pallas kernels, exchange(): pl.pallas_call(exchange_kernel, out_shape=(pltpu.VMEM((SOURCES + 1, ROWS,...  26.2 us
    pallas_call x1, Pallas kernels, make_field(): pl.pallas_call(field_kernel, out_shape=(jax.ShapeDtypeStruct((CX, CY, CZ)...  9.66 us

profile of v7, /device:TPU:1, one launch (start us, length us, event | category | flops | bytes accessed | tf_op | source)
XLA Modules:
  0.0 37.2 jit_solution(1461286926303357413)
XLA Ops:
  1.3 26.2 %exchange_atoms.1 = (f32[28,33,128]{2,1,0:T(8,128)S(1)}, s32[32,128]{1,0:T(8,128)S(1)}, f32[4,144,256]{2,1,0:T(8,128)S(1)}, bf16[8,512,256]{2,1,0:T(8,128)(2,1)S(1)}) custom-call(f32[3,1024]{1,0:T(4,128)} %pos_in.1, f32[8,128]{1,0:T(8,128)} %bitcast.1, s32[3,8]{1,0:T(4,128)} %anchor_in.1, s32[8]{0:T(128)} %atoms_in.1, s32[1]{0:T(128)S(6)} %copy.8.blocks_in, ...), custom_call_target="tpu_custom_call" | custom-call | tf_op jit(solution)/shard_map/exchange_atoms/pallas_call | solution.py:604
  27.5 9.7 %field_and_forces.1 = (f32[24,24,128]{2,1,0:T(8,128)}, f32[3,1024]{1,0:T(4,128)}) custom-call(s32[32,128]{1,0:T(8,128)S(1)} %get-tuple-element.6.meta_in, f32[28,33,128]{2,1,0:T(8,128)S(1)} %get-tuple-element.7.atoms, f32[4,144,256]{2,1,0:T(8,128)S(1)} %get-tuple-element.8.near_in, bf16[8,512,256]{2,1,0:T(8,128)(2,1)S(1)} %get-tuple-element.9.rights), custom_call_target="tpu_custom_call" | custom-call | tf_op jit(solution)/shard_map/field_and_forces/pallas_call | solution.py:212
